TPU v7x, 32 devices: a whole 2x2x4 slice. The times are simulated.
32 devices in a mesh: group: 2 (over x), inst: 4 (over z), tp: 4 (over y, core).
Axes of the slice: x: 2, y: 2, z: 4, core: 2. Of those that a mesh axis runs over, the one named last changes fastest.
Arguments:
- queries: bfloat16 [2048, 2048], P(('group', 'inst'), 'tp'), parts along dimension 0, may hold values from -12 to 12
- new_kv: bfloat16 [4, 2048, 256], P('tp', ('group', 'inst')), parts along dimension 1, may hold values from -12 to 12
- kv_pool: bfloat16 [4, 1024, 128, 256], P('tp', ('group', 'inst')), parts along dimension 1, may hold values from -4 to 4
- out_weight: bfloat16 [2048, 8192], P('tp'), may hold values from -0.5 to 0.5
- lengths: int32 [256], P('group'), parts along dimension 0, may hold values from 1 to 4, as said below
- page_table: int32 [256, 4], P(('group', 'inst')), parts along dimension 0, may hold values from 0 to 127, as said below
- migration: int32 [24, 4], P('group'), parts along dimension 0, may hold values from 0 to 31, as said below
Outputs:
- mixed: bfloat16 [2048, 8192], P(('group', 'inst'), 'tp'), parts along dimension 0
There are 2 independent parts, one for each index of `group`. A program takes and returns all parts, laid end to end along the dimension named above; an argument that names none is the same for every part. Nothing has to cross between parts.
Inputs may be any that keep to these rules, and one draw needn't show every extreme that they name: context lengths in whole pages of 128 tokens; some request has 4 pages in every draw. `page_table`: row g lists the pages of request g in the pool of its home instance g // 32; the entries of one instance's requests are all different. `migration`: each row moves one request; each instance hands exactly 3 of its requests to other instances and takes exactly 3 in, into the slots that its own departing requests leave; at most one request goes from one instance to another.
All inputs are finite; a program needn't handle non-finite values.
Results may differ from a plain program's by a relative error of at most 0.0057.
Values may be sent and summed in bfloat16 or wider, within the bound.
No kernel may reach another device: no remote copies, remote signals or barrier semaphores. Data moves between devices by JAX's collectives and lax.ppermute only.
A program may use at most 128 MiB of HBM per device.

v0:
```python
import jax
import jax.numpy as jnp
from jax import lax
from jax.sharding import PartitionSpec as P


def attend(query_heads, context, context_len, new_tokens):
    head_dim = query_heads.shape[-1]
    step_count = query_heads.shape[1]
    scale = 1.0 / head_dim**0.5
    score_ctx = (
        jnp.einsum(
            "ntqd,nkd->ntqk",
            query_heads,
            context[:, :, :head_dim],
            preferred_element_type=jnp.float32,
        )
        * scale
    )
    positions = jnp.arange(context.shape[1], dtype=jnp.int32)
    live = positions[None, :] < context_len[:, None]
    score_ctx = jnp.where(live[:, None, None, :], score_ctx, jnp.float32(-1e30))
    score_new = (
        jnp.einsum(
            "ntqd,nud->ntqu",
            query_heads,
            new_tokens[:, :, :head_dim],
            preferred_element_type=jnp.float32,
        )
        * scale
    )
    causal = (
        jnp.arange(step_count, dtype=jnp.int32)[None, :]
        <= jnp.arange(step_count, dtype=jnp.int32)[:, None]
    )
    score_new = jnp.where(causal[None, :, None, :], score_new, jnp.float32(-1e30))
    row_max = jnp.maximum(jnp.max(score_ctx, axis=-1), jnp.max(score_new, axis=-1))
    exp_ctx = jnp.exp(score_ctx - row_max[..., None])
    exp_new = jnp.exp(score_new - row_max[..., None])
    row_total = jnp.sum(exp_ctx, axis=-1) + jnp.sum(exp_new, axis=-1)
    weight_ctx = (exp_ctx / row_total[..., None]).astype(jnp.bfloat16)
    weight_new = (exp_new / row_total[..., None]).astype(jnp.bfloat16)
    result = jnp.einsum(
        "ntqk,nkd->ntqd", weight_ctx, context[:, :, head_dim:], preferred_element_type=jnp.float32
    )
    result = result + jnp.einsum(
        "ntqu,nud->ntqd",
        weight_new,
        new_tokens[:, :, head_dim:],
        preferred_element_type=jnp.float32,
    )
    return result.astype(jnp.bfloat16).reshape(
        query_heads.shape[0], step_count, query_heads.shape[2] * head_dim
    )


def pick_lengths(lengths, wanted):
    match = jnp.arange(lengths.shape[0], dtype=jnp.int32)[None, :] == wanted[:, None]
    return jnp.sum(jnp.where(match, lengths[None, :], 0), axis=1)


def on_device(queries, new_kv, kv_pool, out_weight, lengths, page_table, migration):
    inst_count = lax.axis_size("inst")
    own_index = lax.axis_index("inst")
    slot_count, page_count = page_table.shape
    step_count = queries.shape[0] // slot_count
    head_dim = new_kv.shape[2] // 2
    head_count = queries.shape[1] // head_dim
    width = head_count * head_dim
    page_pool = kv_pool[0]
    page_len = page_pool.shape[1]
    context_span = page_count * page_len
    query_heads = queries.reshape(slot_count, step_count, head_count, head_dim)
    new_tokens = new_kv[0].reshape(slot_count, step_count, 2 * head_dim)
    source = migration[:, 0]
    home_slot = migration[:, 1]
    target = migration[:, 2]
    target_slot = migration[:, 3]
    peers = jnp.arange(inst_count, dtype=jnp.int32)
    arrive = (target[None, :] == own_index) & (source[None, :] == peers[:, None])
    depart = (source[None, :] == own_index) & (target[None, :] == peers[:, None])
    arrive_any = jnp.any(arrive, axis=1)
    arrive_slot = jnp.sum(jnp.where(arrive, target_slot[None, :], 0), axis=1)
    arrive_home = jnp.sum(jnp.where(arrive, home_slot[None, :], 0), axis=1)
    depart_any = jnp.any(depart, axis=1)
    depart_slot = jnp.sum(jnp.where(depart, home_slot[None, :], 0), axis=1)
    arrive_len = pick_lengths(lengths, peers * slot_count + arrive_home) * page_len
    slot_ids = jnp.arange(slot_count, dtype=jnp.int32)
    local_len = pick_lengths(lengths, own_index * slot_count + slot_ids) * page_len
    own_rows = source == own_index
    vacated = jnp.any(own_rows[None, :] & (home_slot[None, :] == slot_ids[:, None]), axis=1)
    home_context = page_pool[page_table].reshape(slot_count, context_span, 2 * head_dim)
    resident = attend(query_heads, home_context, local_len, new_tokens)
    outgoing = page_pool[page_table[depart_slot]].reshape(inst_count, 1, context_span, 2 * head_dim)
    outgoing = jnp.where(depart_any[:, None, None, None], outgoing, jnp.zeros_like(outgoing))
    query_in = query_heads[arrive_slot]
    tokens_in = new_tokens[arrive_slot]
    received = lax.all_to_all(outgoing, "inst", split_axis=0, concat_axis=0, tiled=True)
    item_count = received.shape[1]
    context = received.reshape(inst_count * item_count, context_span, 2 * head_dim)
    answer = attend(
        jnp.repeat(query_in, item_count, axis=0),
        context,
        jnp.repeat(arrive_len, item_count, axis=0),
        jnp.repeat(tokens_in, item_count, axis=0),
    )
    arrived = answer.reshape(inst_count, item_count, step_count, width)
    arrived = arrived[:, 0]
    placement = (arrive_any[None, :] & (arrive_slot[None, :] == slot_ids[:, None])).astype(
        jnp.bfloat16
    )
    placed = jnp.einsum(
        "sn,ntc->stc", placement, arrived, preferred_element_type=jnp.float32
    ).astype(jnp.bfloat16)
    attended = jnp.where(vacated[:, None, None], placed, resident).reshape(
        slot_count * step_count, width
    )
    column_count = out_weight.shape[1] // lax.axis_size("tp")
    partial_sum = jnp.dot(attended, out_weight, preferred_element_type=jnp.float32)
    summed = lax.psum(partial_sum, "tp")
    mixed = lax.dynamic_slice_in_dim(summed, lax.axis_index("tp") * column_count, column_count, 1)
    return mixed.astype(jnp.bfloat16)


def solution(mesh):
    placed = (
        P(("group", "inst"), "tp"),
        P("tp", ("group", "inst"), None),
        P("tp", ("group", "inst"), None, None),
        P("tp", None),
        P("group"),
        P(("group", "inst"), None),
        P("group", None),
    )
    return jax.shard_map(
        on_device, mesh=mesh, in_specs=placed, out_specs=P(("group", "inst"), "tp"), check_vma=False
    )
```

profile of v0, /device:TPU:0, one launch (start us, length us, event | category | flops | bytes accessed | tf_op | source)
XLA Modules:
  0.0 199.4 jit_solution(4055378209105462939)
XLA Ops:
  0.0 0.0 copy-start
  0.0 0.8 slice_bitcast_fusion.17
  0.8 0.8 broadcast_compare_fusion
  1.6 0.1 fusion.37
  1.7 0.2 select_reduce_fusion.3
  1.9 0.8 copy.27
  2.7 0.6 gather_fusion.1
  3.2 0.1 reshape.202
  3.3 4.0 %gather_fusion.2 = bf16[16,128,256]{2,1,0:T(8,128)(2,1)S(1)} fusion(bf16[128,128,256]{2,1,0:T(8,128)(2,1)} %bitcast.110, s32[1024]{0:T(1024)S(1)} %pad_clamp_fusion.1), kind=kCustom, calls=%fused_computation.2 | custom fusion | bytes 2097216 | tf_op jit(solution)/shard_map/gather | solution.py:94
  7.3 0.0 copy-start.3
  7.3 0.0 copy-start.4
  7.3 1.1 broadcast_select_fusion
  8.5 6.3 %all-to-all-start = ((bf16[4,1,512,256]{3,2,1,0:T(8,128)(2,1)}), bf16[4,1,512,256]{3,2,1,0:T(8,128)(2,1)S(1)}, u32[]{:S(2)}, u32[]{:S(2)}) async-start(bf16[4,1,512,256]{3,2,1,0:T(8,128)(2,1)} %broadcast_select_fusion), calls=%async_computation | async-start | bytes 2097152 | tf_op jit(solution)/shard_map/all_to_all | solution.py:98
  14.8 0.0 copy-done.3
  14.8 0.0 copy-done.4
  14.8 0.2 select_reduce_fusion
  15.0 0.1 copy.30
  15.1 0.1 reshape.218
  15.2 0.1 iota_compare_fusion
  15.3 0.0 copy-start.2
  15.3 10.0 %gather_fusion.4 = bf16[128,128,256]{2,1,0:T(8,128)(2,1)} fusion(bf16[128,128,256]{2,1,0:T(8,128)(2,1)} %bitcast.111, s32[1024]{0:T(1024)S(1)} %pad_clamp_fusion), kind=kCustom, calls=%fused_computation.4 | custom fusion | bytes 16777728 | tf_op jit(solution)/shard_map/gather | solution.py:92
  25.3 0.0 copy-done
  25.3 1.3 fusion.47
  26.6 0.0 copy-start.1
  26.6 3.9 %bitcast_reduce_fusion = (f32[32,8,4]{1,2,0:T(4,128)S(1)}, f32[32,512,8,4]{1,2,3,0:T(8,128)S(1)}) fusion(pred[32,512]{1,0:T(8,128)(4,1)S(1)} %iota_compare_fusion, bf16[256,512]{1,0:T(8,128)(2,1)S(1)} %copy-done, bf16[32,512,256]{2,1,0:T(8,128)(2,1)} %bitcast.112), kind=kOutput, calls=%fused_computation.10 | convolution fusion | flops 135789568 | bytes 6574080 | tf_op jit(solution)/shard_map/ntqd,nkd->ntqk/dot_general | solution.py:12
  30.5 0.2 fusion.17
  30.8 0.8 fusion.3
  31.6 0.0 copy-done.1
  31.7 1.1 fusion
  32.7 0.5 gather_fusion.3
  33.3 0.6 gather_fusion
  33.8 0.3 fusion.5
  34.2 0.1 copy.32
  34.3 0.1 reshape.182
  34.4 0.1 fusion.46
  34.5 0.2 select_reduce_fusion.2
  34.7 0.1 fusion.31
  34.8 0.1 iota_compare_fusion.2
  34.9 0.3 fusion.49
  35.2 5.3 %all-to-all-done = bf16[4,1,512,256]{3,2,1,0:T(8,128)(2,1)S(1)} async-done(((bf16[4,1,512,256]{3,2,1,0:T(8,128)(2,1)}), bf16[4,1,512,256]{3,2,1,0:T(8,128)(2,1)S(1)}, u32[]{:S(2)}, u32[]{:S(2)}) %all-to-all-start) | async-done | bytes 1048608 | tf_op jit(solution)/shard_map/all_to_all | solution.py:98
  40.5 0.4 fusion.48
  40.9 0.2 fusion.23
  41.1 0.3 fusion.16
  41.4 0.2 fusion.10
  41.6 0.4 fusion.7
  42.0 9.0 %fusion.18 = f32[256,8192]{1,0:T(8,128)} fusion(bf16[512,8192]{1,0:T(8,128)(2,1)} %param.10, bf16[32,8,512]{2,0,1:T(8,128)(2,1)S(1)} %fusion.7), kind=kOutput, calls=%fused_computation.41 | convolution fusion | flops 2147483648 | bytes 17039360 | tf_op jit(solution)/shard_map/dot_general | solution.py:119
  51.0 146.1 %all-reduce.1 = bf16[256,8192]{1,0:T(8,128)(2,1)} all-reduce(f32[256,8192]{1,0:T(8,128)} %fusion.18), channel_id=1, replica_groups=mesh['group'=2,'inst'=4,'tp'=4] {'tp'}, use_global_device_ids=true, to_apply=%region_16.17 | all-reduce | flops 2097152 | bytes 12582912 | tf_op jit(solution)/shard_map/psum | solution.py:120
  197.1 2.3 %dynamic-slice_convert_fusion = bf16[256,2048]{1,0:T(8,128)(2,1)} fusion(bf16[256,8192]{1,0:T(8,128)(2,1)} %all-reduce.1, s32[]{:T(128)S(6)} %select_n.106), kind=kLoop, calls=%fused_computation.12 | loop fusion | bytes 2097156 | tf_op jit(solution)/shard_map/convert_element_type | solution.py:122
  (18 shorter events, 0.2 us)
Async XLA Ops:
  0.0 25.3 %copy-start = (bf16[256,512]{1,0:T(8,128)(2,1)S(1)}, bf16[256,512]{1,0:T(8,128)(2,1)}, u32[]{:S(2)}) copy-start(bf16[256,512]{1,0:T(8,128)(2,1)} %param.7) | copy-start | bytes 786436
  7.3 7.5 %copy-start.3 = (s32[32,4]{0,1:T(4,128)S(1)}, s32[32,4]{0,1:T(4,128)}, u32[]{:S(2)}) copy-start(s32[32,4]{0,1:T(4,128)} %param.12) | copy-start | bytes 1540
  7.3 7.5 %copy-start.4 = (s32[128]{0:T(128)S(1)}, s32[128]{0:T(128)}, u32[]{:S(2)}) copy-start(s32[128]{0:T(128)} %param.11) | copy-start | bytes 1540
  8.5 32.0 %all-to-all-start = ((bf16[4,1,512,256]{3,2,1,0:T(8,128)(2,1)}), bf16[4,1,512,256]{3,2,1,0:T(8,128)(2,1)S(1)}, u32[]{:S(2)}, u32[]{:S(2)}) async-start(bf16[4,1,512,256]{3,2,1,0:T(8,128)(2,1)} %broadcast_select_fusion), calls=%async_computation | async-start | bytes 2097152 | tf_op jit(solution)/shard_map/all_to_all | solution.py:98
  15.3 10.0 %copy-start.2 = (bf16[1,256,256]{2,1,0:T(8,128)(2,1)S(1)}, bf16[1,256,256]{2,1,0:T(8,128)(2,1)}, u32[]{:S(2)}) copy-start(bf16[1,256,256]{2,1,0:T(8,128)(2,1)} %param.8) | copy-start | bytes 393220
  26.6 5.0 %copy-start.1 = (bf16[128,128,256]{2,1,0:T(8,128)(2,1)S(1)}, bf16[128,128,256]{2,1,0:T(8,128)(2,1)}, u32[]{:S(2)}) copy-start(bf16[128,128,256]{2,1,0:T(8,128)(2,1)} %gather_fusion.4) | copy-start | bytes 25165828
where the time goes:
time: 200 us; the launch traced here: 199 us
  blocking collectives  146 us (73%)
  local copies, waits for them, and re-layouts  20.1 us (10%)
  matrix products  17 us (8%)
  starting transfers between devices  6.32 us (3%)
  waiting for transfers between devices  5.34 us (3%)
  other arithmetic  4.3 us (2%)
    psum x1, blocking collectives, on_device(): summed = lax.psum(partial_sum, 'tp')  146 us
    gather x1, local copies, waits for them, and re-layouts, on_device(): page_pool[page_table].reshape(slot_count, context_span, 2 * head_dim)  10 us
    dot_general x1, matrix products, on_device(): jnp.dot(attended, out_weight, preferred_element_type=jnp.float32)  9.01 us
    all_to_all x1, starting transfers between devices, on_device(): lax.all_to_all(outgoing, 'inst', split_axis=0, concat_axis=0, tiled=True)  6.32 us
    all_to_all x1, waiting for transfers between devices, on_device(): lax.all_to_all(outgoing, 'inst', split_axis=0, concat_axis=0, tiled=True)  5.34 us
    dot_general x2, matrix products, attend(): jnp.einsum('ntqd,nkd->ntqk', query_heads, context[:, :, :head_dim], prefe...  4.25 us
  transfers between devices with their start and end apart: 1, of which 1 were waited for; matrix products, arithmetic and copies ran while one was open for 10% of the time, Pallas kernels for 0%

commit v1 on v0

v1 whole, which is shorter than its diff:
```python
import functools

import jax
import jax.numpy as jnp
from jax import lax
from jax.experimental import pallas as pl
from jax.experimental.pallas import tpu as pltpu
from jax.sharding import PartitionSpec as P

LOG2E = 1.4426950408889634
MASKED = -1e30
GROUP = 8

VMEM = pl.BlockSpec(memory_space=pltpu.VMEM)
SMEM = pl.BlockSpec(memory_space=pltpu.SMEM)
HBM = pl.BlockSpec(memory_space=pltpu.HBM)


def contract_last(a, b):
    return lax.dot_general(a, b, (((1,), (1,)), ((), ())), preferred_element_type=jnp.float32)


def attend_group(queries, tokens, contexts, live_lengths, step_count):
    count = len(queries)
    head_dim = tokens[0].shape[1] // 2
    head_count = queries[0].shape[1] // head_dim
    rows = head_count * step_count
    gain = LOG2E / head_dim**0.5
    stacked = jnp.concatenate(
        [
            query[:, h * head_dim : (h + 1) * head_dim]
            for query in queries
            for h in range(head_count)
        ],
        axis=0,
    ).astype(jnp.bfloat16)
    tokens = jnp.concatenate(tokens, axis=0).astype(jnp.bfloat16)
    score_new = contract_last(stacked, tokens[:, :head_dim])
    row_ids = lax.broadcasted_iota(jnp.int32, score_new.shape, 0)
    column_ids = lax.broadcasted_iota(jnp.int32, score_new.shape, 1)
    allowed = (row_ids // rows == column_ids // step_count) & (
        column_ids % step_count <= row_ids % step_count
    )
    score_new = jnp.where(allowed, score_new, MASKED)
    new_max = jnp.max(score_new, axis=1, keepdims=True)
    maxima, scores = [], []
    for g in range(count):
        keys = jnp.concatenate([page[:, :head_dim] for page in contexts[g]], axis=0)
        score = contract_last(stacked[g * rows : (g + 1) * rows], keys)
        position = lax.broadcasted_iota(jnp.int32, score.shape, 1)
        score = jnp.where(position < live_lengths[g], score, MASKED)
        scores.append(score)
        maxima.append(
            jnp.maximum(
                jnp.max(score, axis=1, keepdims=True), new_max[g * rows : (g + 1) * rows]
            )
        )
    exp_new = jnp.exp2((score_new - jnp.concatenate(maxima, axis=0)) * gain)
    new_total = jnp.sum(exp_new, axis=1, keepdims=True)
    results, inverses = [], []
    for g in range(count):
        exp_ctx = jnp.exp2((scores[g] - maxima[g]) * gain)
        total = jnp.sum(exp_ctx, axis=1, keepdims=True) + new_total[g * rows : (g + 1) * rows]
        inverse = 1.0 / total
        inverses.append(inverse)
        values = jnp.concatenate([page[:, head_dim:] for page in contexts[g]], axis=0)
        results.append(
            jnp.dot(
                (exp_ctx * inverse).astype(jnp.bfloat16),
                values,
                preferred_element_type=jnp.float32,
            )
        )
    weight_new = (exp_new * jnp.concatenate(inverses, axis=0)).astype(jnp.bfloat16)
    result = jnp.concatenate(results, axis=0) + jnp.dot(
        weight_new, tokens[:, head_dim:], preferred_element_type=jnp.float32
    )
    return [
        jnp.concatenate(
            [
                result[g * rows + h * step_count : g * rows + (h + 1) * step_count]
                for h in range(head_count)
            ],
            axis=1,
        )
        for g in range(count)
    ]


def route_of(migration, own_index, peer, arriving):
    ours, theirs, slot_row = (2, 0, 3) if arriving else (0, 2, 1)
    slot = jnp.int32(-1)
    for row in range(migration.shape[1]):
        match = (migration[ours, row] == own_index) & (migration[theirs, row] == peer)
        slot = jnp.where(match, migration[slot_row, row], slot)
    return slot


def arrivals_of(migration, inst_count):
    me = lax.axis_index("inst")
    return [
        route_of(migration, me, lax.rem(me + shift, inst_count), True)
        for shift in range(1, inst_count)
    ]


def write_order(migration, inst_count, slot_count, order):
    incoming = migration.shape[1] // inst_count
    kept = slot_count - incoming
    arrivals = arrivals_of(migration, inst_count)
    found = jnp.int32(0)
    for shift, slot in enumerate(arrivals):

        @pl.when((slot >= 0) & (found < incoming))
        def _():
            order[kept + found] = slot
            order[slot_count + found] = shift

        found = found + (slot >= 0).astype(jnp.int32)
    position = jnp.int32(0)
    for slot in range(slot_count):
        moved = jnp.bool_(False)
        for arrival in arrivals:
            moved = moved | (arrival == slot)
        stays = jnp.logical_not(moved) & (position < kept)

        @pl.when(stays)
        def _():
            order[position] = slot

        position = position + stays.astype(jnp.int32)


def pack_kernel(inst_count, migration, queries, new_tokens, after, *outs):
    width = queries.shape[2]
    for out, slot in zip(outs, arrivals_of(migration, inst_count)):
        safe = jnp.maximum(slot, 0)
        out[:, :width] = queries[safe]
        out[:, width:] = new_tokens[safe]


def away_kernel(inst_count, lengths, page_table, migration, after, *refs):
    count = inst_count - 1
    received, pool, outs = refs[:count], refs[count], refs[count + 1 :]
    page_count, slot_count = page_table.shape
    page_len = pool.shape[1]
    me = lax.axis_index("inst")
    step_count, width = outs[0].shape
    live, contexts = [], []
    for k in range(count):
        peer = lax.rem(me + inst_count - (k + 1), inst_count)
        slot = jnp.maximum(route_of(migration, me, peer, False), 0)
        live.append(lengths[me * slot_count + slot] * page_len)
        contexts.append([pool.at[page_table[j, slot]] for j in range(page_count)])
    result = attend_group(
        [ref[:, :width].astype(jnp.float32) for ref in received],
        [ref[:, width:].astype(jnp.float32) for ref in received],
        contexts,
        live,
        step_count,
    )
    for k in range(count):
        outs[k][...] = result[k].astype(jnp.bfloat16)


def attend_positions(positions, order, lengths, page_table, queries, new_tokens, pool):
    page_count, slot_count = page_table.shape
    page_len = pool.shape[1]
    own_first = lax.axis_index("inst") * slot_count
    slots = [order[position] for position in positions]
    return attend_group(
        [queries[slot].astype(jnp.float32) for slot in slots],
        [new_tokens[slot].astype(jnp.float32) for slot in slots],
        [[pool.at[page_table[j, slot]] for j in range(page_count)] for slot in slots],
        [lengths[own_first + slot] * page_len for slot in slots],
        queries.shape[1],
    )


def store_rows(rows, attended):
    step_count = rows[0].shape[0]
    for pair in range(0, len(rows), 2):
        attended[pair * step_count : (pair + 2) * step_count, :] = jnp.concatenate(
            rows[pair : pair + 2], axis=0
        ).astype(jnp.bfloat16)


def project_far(attended, far_weight, keep, send):
    core = lax.rem(lax.axis_index("tp"), 2)
    chips = lax.axis_size("tp") // 2
    columns = far_weight.shape[1] // (2 * chips - 2)
    tile = min(512, columns)
    rows = attended[...]
    for target, side in ((send, 1 - core), (keep, core)):
        for d in range(chips - 1):
            for j in range(0, columns, tile):
                start = pl.multiple_of((2 * d + side) * columns + j, tile)
                target[:, d * columns + j : d * columns + j + tile] = jnp.dot(
                    rows, far_weight[:, pl.ds(start, tile)], preferred_element_type=jnp.float32
                ).astype(target.dtype)


def first_kernel(
    inst_count, migration, lengths, page_table, queries, new_tokens, pool, weight,
    attended, keep, send, order, local_pool, far_weight, page_sems, weight_sems,
):
    page_count, slot_count = page_table.shape
    count = attended.shape[0] // queries.shape[1]
    own_tp = lax.axis_index("tp")
    chips = lax.axis_size("tp") // 2
    pair_columns = weight.shape[1] // chips
    write_order(migration, inst_count, slot_count, order)

    def start_pages(position):
        slot = order[position]
        for j in range(page_count):
            page = page_table[j, slot]
            pltpu.make_async_copy(
                pool.at[page], local_pool.at[page], page_sems.at[position]
            ).start()

    def wait_pages(position):
        pltpu.make_async_copy(
            pool.at[pl.ds(0, page_count)],
            local_pool.at[pl.ds(0, page_count)],
            page_sems.at[position],
        ).wait()

    def weight_copy(d):
        chip = lax.rem(own_tp // 2 + d, chips)
        start = pl.multiple_of(chip * pair_columns, pair_columns)
        return pltpu.make_async_copy(
            weight.at[:, pl.ds(start, pair_columns)],
            far_weight.at[:, pl.ds((d - 1) * pair_columns, pair_columns)],
            weight_sems.at[d - 1],
        )

    for position in range(count):
        start_pages(position)
    for d in range(1, chips):
        weight_copy(d).start()
    pl.loop(count, slot_count)(start_pages)
    rows = []
    for base in range(0, count, GROUP):
        positions = range(base, min(base + GROUP, count))
        for position in positions:
            wait_pages(position)
        rows += attend_positions(
            positions, order, lengths, page_table, queries, new_tokens, local_pool
        )
    store_rows(rows, attended)
    for d in range(1, chips):
        weight_copy(d).wait()
    project_far(attended, far_weight, keep, send)
    pl.loop(count, slot_count)(wait_pages)


def chunk_kernel(
    first_position, order, lengths, page_table, queries, new_tokens, pool, far_weight, after, *refs
):
    answers, (attended, keep, send) = refs[:-3], refs[-3:]
    slot_count = page_table.shape[1]
    count = attended.shape[0] // queries.shape[1]
    local = count - (order.shape[0] - slot_count if answers else 0)
    rows = []
    for base in range(0, local, GROUP):
        positions = range(first_position + base, first_position + min(base + GROUP, local))
        rows += attend_positions(positions, order, lengths, page_table, queries, new_tokens, pool)
    for m in range(count - local):
        chosen = order[slot_count + m]
        row = answers[0][...].astype(jnp.float32)
        for k in range(1, len(answers)):
            row = jnp.where(chosen == k, answers[k][...].astype(jnp.float32), row)
        rows.append(row)
    store_rows(rows, attended)
    project_far(attended, far_weight, keep, send)


def own_kernel(weight, *refs):
    attended, (keep, send, near_weight, sems) = refs[:-4], refs[-4:]
    rows = jnp.concatenate([ref[...] for ref in attended], axis=0)
    core = lax.rem(lax.axis_index("tp"), 2)
    chip = lax.axis_index("tp") // 2
    columns = keep.shape[1]
    copies = []
    for n, side in enumerate((1 - core, core)):
        start = pl.multiple_of((chip * 2 + side) * columns, columns)
        copies.append(
            pltpu.make_async_copy(
                weight.at[:, pl.ds(start, columns)], near_weight.at[n], sems.at[n]
            )
        )
        copies[n].start()
    tile = min(512, columns)
    for n, target in enumerate((send, keep)):
        copies[n].wait()
        for j in range(0, columns, tile):
            target[:, j : j + tile] = jnp.dot(
                rows, near_weight[n, :, j : j + tile], preferred_element_type=jnp.float32
            ).astype(target.dtype)


def final_kernel(step_count, part_count, order, keep, mate, *refs):
    out = refs[-1]
    pair = 2 * step_count
    at = 0
    for chunk in range(0, len(refs) - 1, part_count):
        parts = refs[chunk : chunk + part_count]
        for base in range(0, parts[0].shape[0], pair):
            total = keep[at : at + pair, :] + mate[at : at + pair, :].astype(jnp.float32)
            for part in parts:
                total = total + part[base : base + pair, :].astype(jnp.float32)
            total = total.astype(jnp.bfloat16)
            for half in range(2):
                out[order[at // step_count + half]] = total[
                    half * step_count : (half + 1) * step_count
                ]
            at += pair


def chunk_sizes(slot_count):
    large = (slot_count * 3 // 16) * 2
    return [large, large, slot_count - 2 * large]


def on_device(queries, new_kv, kv_pool, out_weight, lengths, page_table, migration):
    inst_count = lax.axis_size("inst")
    tp_count = lax.axis_size("tp")
    chips = tp_count // 2
    slot_count, page_count = page_table.shape
    row_count, width = queries.shape
    step_count = row_count // slot_count
    queries = queries.reshape(slot_count, step_count, width)
    new_tokens = new_kv[0].reshape(slot_count, step_count, new_kv.shape[2])
    pool = kv_pool[0]
    columns = out_weight.shape[1] // tp_count
    incoming = migration.shape[0] // inst_count
    page_table = page_table.T
    migration = migration.T
    others = inst_count - 1
    limit = pltpu.CompilerParams(vmem_limit_bytes=32 * 2**20)
    wide_limit = pltpu.CompilerParams(vmem_limit_bytes=40 * 2**20)
    light = pl.CostEstimate(flops=1, bytes_accessed=1, transcendentals=0)
    bf16, f32 = jnp.bfloat16, jnp.float32
    shape = jax.ShapeDtypeStruct

    swap = [(t, t ^ 1) for t in range(tp_count)]
    forward = [[(i, (i + k) % inst_count) for i in range(inst_count)] for k in range(inst_count)]
    far = (chips - 1) * columns
    arrived = []

    def chunk_shapes(count):
        rows = count * step_count
        return [shape((rows, width), bf16), shape((rows, far), f32), shape((rows, far), bf16)]

    def hold(value, until):
        return pl.pallas_call(
            lambda *refs: None,
            out_shape=shape(value.shape, value.dtype),
            in_specs=[HBM] * (1 + len(until)),
            out_specs=HBM,
            input_output_aliases={0: 0},
            cost_estimate=light,
            name="hold",
        )(value, *until)

    def exchange(keep, send):
        mate = lax.ppermute(send, "tp", swap)
        if arrived:
            keep = hold(keep, arrived[-(chips - 1) :])
        summed = (keep + mate.astype(f32)).astype(bf16)
        for d in range(1, chips):
            arrived.append(
                lax.ppermute(
                    summed[:, (d - 1) * columns : d * columns],
                    "tp",
                    [(t, (t + 2 * d) % tp_count) for t in range(tp_count)],
                )
            )
        return summed

    counts = chunk_sizes(slot_count)
    attended, keep, send, order, local_pool, far_weight = pl.pallas_call(
        functools.partial(first_kernel, inst_count),
        out_shape=chunk_shapes(counts[0])
        + [
            shape((slot_count + incoming,), jnp.int32),
            shape(pool.shape, bf16),
            shape((width, 2 * far), bf16),
        ],
        in_specs=[SMEM, SMEM, SMEM, VMEM, VMEM, HBM, HBM],
        out_specs=[VMEM] * 3 + [SMEM, VMEM, VMEM],
        scratch_shapes=[
            pltpu.SemaphoreType.DMA((slot_count,)),
            pltpu.SemaphoreType.DMA((chips - 1,)),
        ],
        compiler_params=wide_limit,
        cost_estimate=light,
        name="attend_first",
    )(migration, lengths, page_table, queries, new_tokens, pool, out_weight)
    chunks = [attended]
    summed = exchange(keep, send)
    packs = pl.pallas_call(
        functools.partial(pack_kernel, inst_count),
        out_shape=[shape((step_count, width + new_tokens.shape[2]), bf16)] * others,
        in_specs=[SMEM, VMEM, VMEM, HBM],
        out_specs=[VMEM] * others,
        compiler_params=limit,
        cost_estimate=light,
        name="pack",
    )(migration, queries, new_tokens, summed)
    received = [lax.ppermute(packs[k - 1], "inst", forward[k]) for k in range(1, inst_count)]
    first = counts[0]
    after = packs[0]
    answers = []
    for count in counts[1:]:
        last = first + count == slot_count
        if last:
            answers = pl.pallas_call(
                functools.partial(away_kernel, inst_count),
                out_shape=[shape((step_count, width), bf16)] * others,
                in_specs=[SMEM, SMEM, SMEM, HBM] + [VMEM] * (others + 1),
                out_specs=[VMEM] * others,
                compiler_params=limit,
                cost_estimate=light,
                name="attend_away",
            )(lengths, page_table, migration, chunks[-1], *received, local_pool)
            answers = [
                lax.ppermute(answers[k - 1], "inst", [(b, a) for a, b in forward[k]])
                for k in range(1, inst_count)
            ]
        attended, keep, send = pl.pallas_call(
            functools.partial(chunk_kernel, first),
            out_shape=chunk_shapes(count),
            in_specs=[SMEM, SMEM, SMEM] + [VMEM] * 4 + [HBM] + [VMEM] * len(answers),
            out_specs=[VMEM] * 3,
            compiler_params=limit,
            cost_estimate=light,
            name="attend_chunk",
        )(order, lengths, page_table, queries, new_tokens, local_pool, far_weight, after, *answers)
        chunks.append(attended)
        after = exchange(keep, send)
        first += count
    keep, send = pl.pallas_call(
        own_kernel,
        out_shape=[shape((row_count, columns), f32), shape((row_count, columns), bf16)],
        in_specs=[HBM] + [VMEM] * len(counts),
        out_specs=[VMEM] * 2,
        scratch_shapes=[
            pltpu.VMEM((2, width, columns), bf16),
            pltpu.SemaphoreType.DMA((2,)),
        ],
        compiler_params=pltpu.CompilerParams(vmem_limit_bytes=54 * 2**20),
        cost_estimate=light,
        name="own_columns",
    )(out_weight, *chunks)
    mate = lax.ppermute(send, "tp", swap)
    out = pl.pallas_call(
        functools.partial(final_kernel, step_count, chips - 1),
        out_shape=shape((slot_count, step_count, columns), bf16),
        in_specs=[SMEM] + [VMEM] * (2 + len(arrived)),
        out_specs=VMEM,
        compiler_params=limit,
        name="final_sum",
    )(order, keep, mate, *arrived)
    return out.reshape(row_count, columns)


def solution(mesh):
    placed = (
        P(("group", "inst"), "tp"),
        P("tp", ("group", "inst"), None),
        P("tp", ("group", "inst"), None, None),
        P("tp", None),
        P("group"),
        P(("group", "inst"), None),
        P("group", None),
    )
    return jax.shard_map(
        on_device, mesh=mesh, in_specs=placed, out_specs=P(("group", "inst"), "tp"), check_vma=False
    )
```

time: 200 us -> 78.6 us (0.39)
  blocking collectives: 146 us -> 0 us
  Pallas kernels: 0 us -> 20.8 us
  matrix products: 17 us -> 0 us
  waiting for transfers between devices: 5.34 us -> 22 us
  starting transfers between devices: 6.32 us -> 13.1 us
    psum x1 -> x0, blocking collectives: 146 us -> none  [on_device(): summed = lax.psum(partial_sum, 'tp')]
    ppermute x0 -> x13, waiting for transfers between devices: none -> 22 us  [the longest x3 10.3 us: exchange(): lax.ppermute(summed[:, (d - 1) * columns:d * columns], 'tp', [(t, (t + 2...]
    pallas_call x0 -> x9, Pallas kernels: none -> 20.8 us  [the longest x1 6.31 us: on_device(): pl.pallas_call(functools.partial(first_kernel, inst_count), out_shape=chu...]
    unnamed x11 -> x50, local copies, waits for them, and re-layouts: 0.79 us -> 19.8 us
    dot_general x10 -> x0, matrix products: 17 us -> none  [the longest x1 9.01 us: on_device(): jnp.dot(attended, out_weight, preferred_element_type=jnp.float32)]
    gather x5 -> x0, local copies, waits for them, and re-layouts: 15.7 us -> none  [the longest x1 10 us: on_device(): page_pool[page_table].reshape(slot_count, context_span, 2 * head_dim)]
    ppermute x0 -> x13, starting transfers between devices: none -> 13.1 us  [the longest x3 5.33 us: exchange(): lax.ppermute(summed[:, (d - 1) * columns:d * columns], 'tp', [(t, (t + 2...]
    all_to_all x1 -> x0, starting transfers between devices: 6.32 us -> none  [on_device(): lax.all_to_all(outgoing, 'inst', split_axis=0, concat_axis=0, tiled=True)]
  transfers between devices with their start and end apart: 1 -> 13, of which waited for: 1 -> 9; matrix products, arithmetic and copies ran while one was open for 10% -> 1% of each run, Pallas kernels for 0% -> 15%
where the time goes in v1:
time: 78.6 us; the launch traced here: 78.2 us
  waiting for transfers between devices  22 us (28%)
  Pallas kernels  20.8 us (26%)
  local copies, waits for them, and re-layouts  19.8 us (25%)
  starting transfers between devices  13.1 us (17%)
  other arithmetic  2.4 us (3%)
    unnamed x50, local copies, waits for them, and re-layouts  19.8 us
    ppermute x3, waiting for transfers between devices, exchange(): lax.ppermute(summed[:, (d - 1) * columns:d * columns], 'tp', [(t, (t + 2...  10.3 us
    pallas_call x1, Pallas kernels, on_device(): pl.pallas_call(functools.partial(first_kernel, inst_count), out_shape=chu...  6.31 us
    pallas_call x1, Pallas kernels, on_device(): pl.pallas_call(own_kernel, out_shape=[shape((row_count, columns), f32), s...  5.41 us
    ppermute x3, starting transfers between devices, exchange(): lax.ppermute(summed[:, (d - 1) * columns:d * columns], 'tp', [(t, (t + 2...  5.33 us
    pallas_call x2, Pallas kernels, on_device(): pl.pallas_call(functools.partial(chunk_kernel, first), out_shape=chunk_sh...  5.18 us
    ppermute x3, waiting for transfers between devices, on_device(): lax.ppermute(packs[k - 1], 'inst', forward[k])  4.81 us
    ppermute x3, starting transfers between devices, on_device(): lax.ppermute(packs[k - 1], 'inst', forward[k])  4.61 us
  transfers between devices with their start and end apart: 13, of which 9 were waited for; matrix products, arithmetic and copies ran while one was open for 1% of the time, Pallas kernels for 15%

profile of v1, /device:TPU:0, one launch (start us, length us, event | category | flops | bytes accessed | tf_op | source)
XLA Modules:
  0.0 78.2 jit_solution(11737995973023011024)
XLA Ops:
  0.0 0.9 %copy-done.5 = bf16[256,512]{1,0:T(8,128)(2,1)S(1)} copy-done((bf16[256,512]{1,0:T(8,128)(2,1)S(1)}, bf16[256,512]{1,0:T(8,128)(2,1)}, u32[]{:S(2)}) %copy-start.5) | copy-done | bytes 262168
  1.0 0.9 %copy-done.8 = bf16[1,256,256]{2,1,0:T(8,128)(2,1)S(1)} copy-done((bf16[1,256,256]{2,1,0:T(8,128)(2,1)S(1)}, bf16[1,256,256]{2,1,0:T(8,128)(2,1)}, u32[]{:S(2)}) %copy-start.8) | copy-done | bytes 131096
  1.9 0.7 copy-done.19
  2.5 0.7 copy-done.21
  3.2 0.7 copy-done.23
  3.9 6.3 %attend_first.1 = (bf16[96,512]{1,0:T(8,128)(2,1)S(1)}, f32[96,2048]{1,0:T(8,128)S(1)}, bf16[96,2048]{1,0:T(8,128)(2,1)S(1)}, s32[35]{0:T(128)S(1)}, bf16[128,12...) custom-call(s32[4,12]{1,0:T(4,128)S(1)} %bitcast.18, s32[128]{0:T(128)S(1)} %copy-done.23, s32[4,32]{1,0:T(4,128)S(1)} %bitcast.14, ...), custom_call_target="tpu_custom_call" | custom-call | flops 1 | bytes 1 | tf_op jit(solution)/shard_map/attend_first/pallas_call | solution.py:383
  10.2 0.5 collective-permute-start
  10.7 1.3 %collective-permute-done = bf16[96,2048]{1,0:T(8,128)(2,1)S(1)} collective-permute-done((bf16[96,2048]{1,0:T(8,128)(2,1)S(1)}, bf16[96,2048]{1,0:T(8,128)(2,1)S(1)}, u32[]{:S(2)}, u32[]{:S(2)}) %collective-permute-start) | collective-permute-done | bytes 393248 | tf_op jit(solution)/shard_map/ppermute | solution.py:368
  12.1 0.1 add_convert_fusion.1.after
  12.2 0.7 pack.1
  12.9 0.0 copy-start.24
  12.9 3.0 %collective-permute-start.1 = (bf16[96,2048]{1,0:T(8,128)(2,1)S(1)}, bf16[96,2048]{1,0:T(8,128)(2,1)S(1)}, u32[]{:S(2)}, u32[]{:S(2)}) collective-permute-start(bf16[96,2048]{1,0:T(8,128)(2,1)S(1)} %add_convert_fusion.1.after), channel_id=1, source_target_pairs={{0,2},{1,3},{2,0},{3,1},{4,6},{5,7},{6,4},{7,5},{8,10},{9,11},{10,... | collective-permute-start | bytes 1179656 | tf_op jit(solution)/shard_map/ppermute | solution.py:374
  15.8 3.0 %attend_chunk.2 = (bf16[96,512]{1,0:T(8,128)(2,1)S(1)}, f32[96,2048]{1,0:T(8,128)S(1)}, bf16[96,2048]{1,0:T(8,128)(2,1)S(1)}) custom-call(s32[35]{0:T(128)S(1)} %get-tuple-element.25.order, s32[128]{0:T(128)S(1)} %copy-done.23, s32[4,32]{1,0:T(4,128)S(1)} %bitcast.15, bf16[32,8,512]{2,1,0:T(8,128)(2,1)S(1)} %bitcast.8, bf16[32,8,256]{2,1,0:T(8,128)(2,1)S(1)} %bitcast.12, ...), custom_call_target="tpu_custom_call" | custom-call | flops 1 | bytes 1 | tf_op jit(solution)/shard_map/attend_chunk/pallas_call | solution.py:432
  18.8 3.3 %copy-done = bf16[128,128,256]{2,1,0:T(8,128)(2,1)} copy-done((bf16[128,128,256]{2,1,0:T(8,128)(2,1)}, bf16[128,128,256]{2,1,0:T(8,128)(2,1)S(1)}, u32[]{:S(2)}) %copy-start) | copy-done | bytes 8388632
  22.1 0.9 %copy-done.7 = f32[96,2048]{1,0:T(8,128)} copy-done((f32[96,2048]{1,0:T(8,128)}, f32[96,2048]{1,0:T(8,128)S(1)}, u32[]{:S(2)}) %copy-start.7) | copy-done | bytes 786456
  23.0 2.3 %collective-permute-done.1.refs_1_.refs_0_ = bf16[96,2048]{1,0:T(8,128)(2,1)S(1)} collective-permute-done((bf16[96,2048]{1,0:T(8,128)(2,1)S(1)}, bf16[96,2048]{1,0:T(8,128)(2,1)S(1)}, u32[]{:S(2)}, u32[]{:S(2)}) %collective-permute-start.1) | collective-permute-done | bytes 393248 | tf_op jit(solution)/shard_map/ppermute | solution.py:374
  25.3 0.8 copy-done.14
  26.0 1.2 %add_convert_fusion.after = bf16[96,2048]{1,0:T(8,128)(2,1)S(1)} fusion(f32[96,2048]{1,0:T(8,128)} %hold.2, bf16[96,2048]{1,0:T(8,128)(2,1)S(1)} %collective-permute-done.2), kind=kLoop, calls=%fused_computation | loop fusion | flops 589824 | bytes 1572864 | tf_op jit(solution)/shard_map/convert_element_type | solution.py:371
  27.2 1.8 %collective-permute-start.10 = (bf16[96,2048]{1,0:T(8,128)(2,1)S(1)}, bf16[96,2048]{1,0:T(8,128)(2,1)S(1)}, u32[]{:S(2)}, u32[]{:S(2)}) collective-permute-start(bf16[96,2048]{1,0:T(8,128)(2,1)S(1)} %add_convert_fusion.after), channel_id=1, source_target_pairs={{0,2},{1,3},{2,0},{3,1},{4,6},{5,7},{6,4},{7,5},{8,10},{9,11},{10,... | collective-permute-start | bytes 1179656 | tf_op jit(solution)/shard_map/ppermute | solution.py:374
  29.0 2.6 %collective-permute-start.4 = (bf16[8,768]{1,0:T(8,128)(2,1)S(1)}, bf16[8,768]{1,0:T(8,128)(2,1)S(1)}, u32[]{:S(2)}, u32[]{:S(2)}) collective-permute-start(bf16[8,768]{1,0:T(8,128)(2,1)S(1)} %get-tuple-element.35), channel_id=1, source_target_pairs={{0,8},{4,12},{8,0},{12,4},{1,9},{5,13},{9,1},{13,5},{2,10},{6,14},... | collective-permute-start | bytes 36872 | tf_op jit(solution)/shard_map/ppermute | solution.py:412
  31.6 1.3 %collective-permute-start.5 = (bf16[8,768]{1,0:T(8,128)(2,1)S(1)}, bf16[8,768]{1,0:T(8,128)(2,1)S(1)}, u32[]{:S(2)}, u32[]{:S(2)}) collective-permute-start(bf16[8,768]{1,0:T(8,128)(2,1)S(1)} %get-tuple-element.36), channel_id=1, source_target_pairs={{0,12},{4,0},{8,4},{12,8},{1,13},{5,1},{9,5},{13,9},{2,14},{6,2},{... | collective-permute-start | bytes 36872 | tf_op jit(solution)/shard_map/ppermute | solution.py:412
  33.0 0.7 collective-permute-start.3
  33.7 1.7 %collective-permute-done.5.refs_2_ = bf16[8,768]{1,0:T(8,128)(2,1)S(1)} collective-permute-done((bf16[8,768]{1,0:T(8,128)(2,1)S(1)}, bf16[8,768]{1,0:T(8,128)(2,1)S(1)}, u32[]{:S(2)}, u32[]{:S(2)}) %collective-permute-start.5) | collective-permute-done | bytes 12320 | tf_op jit(solution)/shard_map/ppermute | solution.py:412
  35.3 3.1 %collective-permute-done.3.refs_0_ = bf16[8,768]{1,0:T(8,128)(2,1)S(1)} collective-permute-done((bf16[8,768]{1,0:T(8,128)(2,1)S(1)}, bf16[8,768]{1,0:T(8,128)(2,1)S(1)}, u32[]{:S(2)}, u32[]{:S(2)}) %collective-permute-start.3) | collective-permute-done | bytes 12320 | tf_op jit(solution)/shard_map/ppermute | solution.py:412
  38.5 3.4 %copy-done.1 = bf16[128,128,256]{2,1,0:T(8,128)(2,1)S(1)} copy-done((bf16[128,128,256]{2,1,0:T(8,128)(2,1)S(1)}, bf16[128,128,256]{2,1,0:T(8,128)(2,1)}, u32[]{:S(2)}) %copy-start.1) | copy-done | bytes 8388632
  41.9 1.3 %attend_away.1 = (bf16[8,512]{1,0:T(8,128)(2,1)S(1)}, bf16[8,512]{1,0:T(8,128)(2,1)S(1)}, bf16[8,512]{1,0:T(8,128)(2,1)S(1)}) custom-call(s32[128]{0:T(128)S(1)} %copy-done.24, s32[4,32]{1,0:T(4,128)S(1)} %bitcast.16, s32[4,12]{1,0:T(4,128)S(1)} %bitcast.20, bf16[96,512]{1,0:T(8,128)(2,1)S(1)} %get-tuple-element.32.after.refs_1_, ...), custom_call_target="tpu_custom_call" | custom-call | flops 1 | bytes 1 | tf_op jit(solution)/shard_map/attend_away/pallas_call | solution.py:419
  43.2 0.6 copy-done.16
  43.8 0.0 collective-permute-start.6
  43.8 0.3 collective-permute-start.7
  44.2 1.7 %collective-permute-start.8 = (bf16[8,512]{1,0:T(8,128)(2,1)S(1)}, bf16[8,512]{1,0:T(8,128)(2,1)S(1)}, u32[]{:S(2)}, u32[]{:S(2)}) collective-permute-start(bf16[8,512]{1,0:T(8,128)(2,1)S(1)} %get-tuple-element.39), channel_id=1, source_target_pairs={{12,0},{0,4},{4,8},{8,12},{13,1},{1,5},{5,9},{9,13},{14,2},{2,6},{... | collective-permute-start | bytes 24584 | tf_op jit(solution)/shard_map/ppermute | solution.py:429
  45.9 1.6 %collective-permute-done.6.refs_0_ = bf16[8,512]{1,0:T(8,128)(2,1)S(1)} collective-permute-done((bf16[8,512]{1,0:T(8,128)(2,1)S(1)}, bf16[8,512]{1,0:T(8,128)(2,1)S(1)}, u32[]{:S(2)}, u32[]{:S(2)}) %collective-permute-start.6) | collective-permute-done | bytes 8224 | tf_op jit(solution)/shard_map/ppermute | solution.py:429
  47.5 0.9 %collective-permute-done.7.refs_1_ = bf16[8,512]{1,0:T(8,128)(2,1)S(1)} collective-permute-done((bf16[8,512]{1,0:T(8,128)(2,1)S(1)}, bf16[8,512]{1,0:T(8,128)(2,1)S(1)}, u32[]{:S(2)}, u32[]{:S(2)}) %collective-permute-start.7) | collective-permute-done | bytes 8224 | tf_op jit(solution)/shard_map/ppermute | solution.py:429
  48.4 1.5 %collective-permute-done.8.refs_2_ = bf16[8,512]{1,0:T(8,128)(2,1)S(1)} collective-permute-done((bf16[8,512]{1,0:T(8,128)(2,1)S(1)}, bf16[8,512]{1,0:T(8,128)(2,1)S(1)}, u32[]{:S(2)}, u32[]{:S(2)}) %collective-permute-start.8) | collective-permute-done | bytes 8224 | tf_op jit(solution)/shard_map/ppermute | solution.py:429
  49.9 2.2 %copy-done.4 = bf16[512,4096]{1,0:T(8,128)(2,1)S(1)} copy-done((bf16[512,4096]{1,0:T(8,128)(2,1)S(1)}, bf16[512,4096]{1,0:T(8,128)(2,1)}, u32[]{:S(2)}) %copy-start.4) | copy-done | bytes 4194328
  52.1 2.2 %attend_chunk.3 = (bf16[64,512]{1,0:T(8,128)(2,1)S(1)}, f32[64,2048]{1,0:T(8,128)S(1)}, bf16[64,2048]{1,0:T(8,128)(2,1)S(1)}) custom-call(s32[35]{0:T(128)S(1)} %get-tuple-element.25.order, s32[128]{0:T(128)S(1)} %copy-done.24, s32[4,32]{1,0:T(4,128)S(1)} %bitcast.17, bf16[32,8,512]{2,1,0:T(8,128)(2,1)S(1)} %bitcast.9, bf16[32,8,256]{2,1,0:T(8,128)(2,1)S(1)} %bitcast.13, ...), custom_call_target="tpu_custom_call" | custom-call | flops 1 | bytes 1 | tf_op jit(solution)/shard_map/attend_chunk/pallas_call | solution.py:432
  54.3 0.8 %copy-done.11 = f32[64,2048]{1,0:T(8,128)} copy-done((f32[64,2048]{1,0:T(8,128)}, f32[64,2048]{1,0:T(8,128)S(1)}, u32[]{:S(2)}) %copy-start.11) | copy-done | bytes 524312
  55.1 0.6 copy-done.18
  55.8 5.4 %own_columns.1 = (f32[256,2048]{1,0:T(8,128)}, bf16[256,2048]{1,0:T(8,128)(2,1)}) custom-call(bf16[512,8192]{1,0:T(8,128)(2,1)} %weight.3, bf16[96,512]{1,0:T(8,128)(2,1)} %copy-done.17, bf16[96,512]{1,0:T(8,128)(2,1)} %copy-done.16, bf16[64,512]{1,0:T(8,128)(2,1)} %copy-done.18), custom_call_target="tpu_custom_call" | custom-call | flops 1 | bytes 1 | tf_op jit(solution)/shard_map/own_columns/pallas_call | solution.py:444
  61.2 0.1 collective-permute-start.9
  61.3 0.5 collective-permute-start.11
  61.8 0.7 copy-done.12
  62.5 1.4 %collective-permute-done.11 = bf16[64,2048]{1,0:T(8,128)(2,1)S(1)} collective-permute-done((bf16[64,2048]{1,0:T(8,128)(2,1)S(1)}, bf16[64,2048]{1,0:T(8,128)(2,1)S(1)}, u32[]{:S(2)}, u32[]{:S(2)}) %collective-permute-start.11) | collective-permute-done | bytes 262176 | tf_op jit(solution)/shard_map/ppermute | solution.py:368
  63.9 1.1 %add_convert_fusion.2 = bf16[64,2048]{1,0:T(8,128)(2,1)S(1)} fusion(f32[64,2048]{1,0:T(8,128)} %hold.3, bf16[64,2048]{1,0:T(8,128)(2,1)S(1)} %collective-permute-done.11), kind=kLoop, calls=%fused_computation.2 | loop fusion | flops 393216 | bytes 1048576 | tf_op jit(solution)/shard_map/convert_element_type | solution.py:371
  65.0 0.6 collective-permute-start.12
  65.6 8.0 %collective-permute-done.12.refs_2_ = bf16[64,2048]{1,0:T(8,128)(2,1)S(1)} collective-permute-done((bf16[64,2048]{1,0:T(8,128)(2,1)S(1)}, bf16[64,2048]{1,0:T(8,128)(2,1)S(1)}, u32[]{:S(2)}, u32[]{:S(2)}) %collective-permute-start.12) | collective-permute-done | bytes 262176 | tf_op jit(solution)/shard_map/ppermute | solution.py:374
  73.7 1.6 %copy-done.10 = f32[256,2048]{1,0:T(8,128)S(1)} copy-done((f32[256,2048]{1,0:T(8,128)S(1)}, f32[256,2048]{1,0:T(8,128)}, u32[]{:S(2)}) %copy-start.10) | copy-done | bytes 2097176
  75.3 1.0 %copy-done.13 = bf16[96,2048]{1,0:T(8,128)(2,1)S(1)} copy-done((bf16[96,2048]{1,0:T(8,128)(2,1)S(1)}, bf16[96,2048]{1,0:T(8,128)(2,1)}, u32[]{:S(2)}) %copy-start.13) | copy-done | bytes 393240
  76.3 1.9 %final_sum.1 = bf16[32,8,2048]{2,1,0:T(8,128)(2,1)} custom-call(s32[35]{0:T(128)S(1)} %get-tuple-element.25.order, f32[256,2048]{1,0:T(8,128)S(1)} %copy-done.10, bf16[256,2048]{1,0:T(8,128)(2,1)S(1)} %collective-permute-done.9.mate, bf16[96,2048]{1,0:T(8,128)(2,1)S(1)} %copy-done.15, bf16[96,2048]{1,0:T(8,128)(2,1)S(1)} %copy-done.13, ...), custom_call_target="tpu_custom_call" | custom-call | tf_op jit(solution)/shard_map/final_sum/pallas_call | solution.py:458
  (40 shorter events, 0.1 us)
Async XLA Ops:
  0.0 0.9 %copy-start.5 = (bf16[256,512]{1,0:T(8,128)(2,1)S(1)}, bf16[256,512]{1,0:T(8,128)(2,1)}, u32[]{:S(2)}) copy-start(bf16[256,512]{1,0:T(8,128)(2,1)} %param.7) | copy-start | bytes 786436
  1.0 0.9 %copy-start.8 = (bf16[1,256,256]{2,1,0:T(8,128)(2,1)S(1)}, bf16[1,256,256]{2,1,0:T(8,128)(2,1)}, u32[]{:S(2)}) copy-start(bf16[1,256,256]{2,1,0:T(8,128)(2,1)} %param.8) | copy-start | bytes 393220
  1.9 0.7 copy-start.19
  2.5 0.7 copy-start.21
  3.2 0.7 copy-start.23
  10.2 8.6 %copy-start.3 = (bf16[512,4096]{1,0:T(8,128)(2,1)}, bf16[512,4096]{1,0:T(8,128)(2,1)S(1)}, u32[]{:S(2)}) copy-start(bf16[512,4096]{1,0:T(8,128)(2,1)S(1)} %get-tuple-element.28.far_weight) | copy-start | bytes 12582916
  10.2 15.1 %copy-start.17 = (bf16[96,512]{1,0:T(8,128)(2,1)}, bf16[96,512]{1,0:T(8,128)(2,1)S(1)}, u32[]{:S(2)}) copy-start(bf16[96,512]{1,0:T(8,128)(2,1)S(1)} %get-tuple-element.26.refs_0_) | copy-start | bytes 294916
  10.2 1.9 %collective-permute-start = (bf16[96,2048]{1,0:T(8,128)(2,1)S(1)}, bf16[96,2048]{1,0:T(8,128)(2,1)S(1)}, u32[]{:S(2)}, u32[]{:S(2)}) collective-permute-start(bf16[96,2048]{1,0:T(8,128)(2,1)S(1)} %get-tuple-element.30), channel_id=1, source_target_pairs={{0,1},{1,0},{2,3},{3,2},{4,5},{5,4},{6,7},{7,6},{8,9},{9,8},{10,11... | collective-permute-start | bytes 1179656 | tf_op jit(solution)/shard_map/ppermute | solution.py:368
  12.8 25.6 %copy-start.20 = (s32[32,4]{0,1:T(4,128)S(1)}, s32[32,4]{0,1:T(4,128)}, u32[]{:S(2)}) copy-start(s32[32,4]{0,1:T(4,128)} %param.12) | copy-start | bytes 1540
  12.9 25.6 %copy-start.22 = (s32[12,4]{0,1:T(4,128)S(1)}, s32[12,4]{0,1:T(4,128)}, u32[]{:S(2)}) copy-start(s32[12,4]{0,1:T(4,128)} %param.13) | copy-start | bytes 580
  12.9 25.6 %copy-start.24 = (s32[128]{0:T(128)S(1)}, s32[128]{0:T(128)}, u32[]{:S(2)}) copy-start(s32[128]{0:T(128)} %lengths.7) | copy-start | bytes 1540
  12.9 12.4 %collective-permute-start.1 = (bf16[96,2048]{1,0:T(8,128)(2,1)S(1)}, bf16[96,2048]{1,0:T(8,128)(2,1)S(1)}, u32[]{:S(2)}, u32[]{:S(2)}) collective-permute-start(bf16[96,2048]{1,0:T(8,128)(2,1)S(1)} %add_convert_fusion.1.after), channel_id=1, source_target_pairs={{0,2},{1,3},{2,0},{3,1},{4,6},{5,7},{6,4},{7,5},{8,10},{9,11},{10,... | collective-permute-start | bytes 1179656 | tf_op jit(solution)/shard_map/ppermute | solution.py:374
  18.8 3.3 %copy-start = (bf16[128,128,256]{2,1,0:T(8,128)(2,1)}, bf16[128,128,256]{2,1,0:T(8,128)(2,1)S(1)}, u32[]{:S(2)}) copy-start(bf16[128,128,256]{2,1,0:T(8,128)(2,1)S(1)} %get-tuple-element.27.pool.refs_3_) | copy-start | bytes 25165828
  22.1 0.9 %copy-start.7 = (f32[96,2048]{1,0:T(8,128)}, f32[96,2048]{1,0:T(8,128)S(1)}, u32[]{:S(2)}) copy-start(f32[96,2048]{1,0:T(8,128)S(1)} %get-tuple-element.33.refs_0_) | copy-start | bytes 2359300
  23.0 27.0 %copy-start.6 = (bf16[256,512]{1,0:T(8,128)(2,1)S(1)}, bf16[256,512]{1,0:T(8,128)(2,1)}, u32[]{:S(2)}) copy-start(bf16[256,512]{1,0:T(8,128)(2,1)} %param.7) | copy-start | bytes 786436
  23.0 27.0 %copy-start.9 = (bf16[1,256,256]{2,1,0:T(8,128)(2,1)S(1)}, bf16[1,256,256]{2,1,0:T(8,128)(2,1)}, u32[]{:S(2)}) copy-start(bf16[1,256,256]{2,1,0:T(8,128)(2,1)} %param.8) | copy-start | bytes 393220
  23.0 3.0 %collective-permute-start.2 = (bf16[96,2048]{1,0:T(8,128)(2,1)S(1)}, bf16[96,2048]{1,0:T(8,128)(2,1)S(1)}, u32[]{:S(2)}, u32[]{:S(2)}) collective-permute-start(bf16[96,2048]{1,0:T(8,128)(2,1)S(1)} %get-tuple-element.34), channel_id=1, source_target_pairs={{0,1},{1,0},{2,3},{3,2},{4,5},{5,4},{6,7},{7,6},{8,9},{9,8},{10,11... | collective-permute-start | bytes 1179656 | tf_op jit(solution)/shard_map/ppermute | solution.py:368
  25.3 0.8 copy-start.14
  27.2 34.5 %collective-permute-start.10 = (bf16[96,2048]{1,0:T(8,128)(2,1)S(1)}, bf16[96,2048]{1,0:T(8,128)(2,1)S(1)}, u32[]{:S(2)}, u32[]{:S(2)}) collective-permute-start(bf16[96,2048]{1,0:T(8,128)(2,1)S(1)} %add_convert_fusion.after), channel_id=1, source_target_pairs={{0,2},{1,3},{2,0},{3,1},{4,6},{5,7},{6,4},{7,5},{8,10},{9,11},{10,... | collective-permute-start | bytes 1179656 | tf_op jit(solution)/shard_map/ppermute | solution.py:374
  29.0 4.6 %collective-permute-start.4 = (bf16[8,768]{1,0:T(8,128)(2,1)S(1)}, bf16[8,768]{1,0:T(8,128)(2,1)S(1)}, u32[]{:S(2)}, u32[]{:S(2)}) collective-permute-start(bf16[8,768]{1,0:T(8,128)(2,1)S(1)} %get-tuple-element.35), channel_id=1, source_target_pairs={{0,8},{4,12},{8,0},{12,4},{1,9},{5,13},{9,1},{13,5},{2,10},{6,14},... | collective-permute-start | bytes 36872 | tf_op jit(solution)/shard_map/ppermute | solution.py:412
  31.6 3.7 %collective-permute-start.5 = (bf16[8,768]{1,0:T(8,128)(2,1)S(1)}, bf16[8,768]{1,0:T(8,128)(2,1)S(1)}, u32[]{:S(2)}, u32[]{:S(2)}) collective-permute-start(bf16[8,768]{1,0:T(8,128)(2,1)S(1)} %get-tuple-element.36), channel_id=1, source_target_pairs={{0,12},{4,0},{8,4},{12,8},{1,13},{5,1},{9,5},{13,9},{2,14},{6,2},{... | collective-permute-start | bytes 36872 | tf_op jit(solution)/shard_map/ppermute | solution.py:412
  33.0 5.5 %collective-permute-start.3 = (bf16[8,768]{1,0:T(8,128)(2,1)S(1)}, bf16[8,768]{1,0:T(8,128)(2,1)S(1)}, u32[]{:S(2)}, u32[]{:S(2)}) collective-permute-start(bf16[8,768]{1,0:T(8,128)(2,1)S(1)} %get-tuple-element.31.after), channel_id=1, source_target_pairs={{0,4},{4,8},{8,12},{12,0},{1,5},{5,9},{9,13},{13,1},{2,6},{6,10},{... | collective-permute-start | bytes 36872 | tf_op jit(solution)/shard_map/ppermute | solution.py:412
  38.5 3.4 %copy-start.1 = (bf16[128,128,256]{2,1,0:T(8,128)(2,1)S(1)}, bf16[128,128,256]{2,1,0:T(8,128)(2,1)}, u32[]{:S(2)}) copy-start(bf16[128,128,256]{2,1,0:T(8,128)(2,1)} %copy-done) | copy-start | bytes 25165828
  41.9 8.1 %copy-start.2 = (bf16[128,128,256]{2,1,0:T(8,128)(2,1)S(1)}, bf16[128,128,256]{2,1,0:T(8,128)(2,1)}, u32[]{:S(2)}) copy-start(bf16[128,128,256]{2,1,0:T(8,128)(2,1)} %copy-done) | copy-start | bytes 25165828
  43.2 0.7 copy-start.16
  43.8 3.7 %collective-permute-start.6 = (bf16[8,512]{1,0:T(8,128)(2,1)S(1)}, bf16[8,512]{1,0:T(8,128)(2,1)S(1)}, u32[]{:S(2)}, u32[]{:S(2)}) collective-permute-start(bf16[8,512]{1,0:T(8,128)(2,1)S(1)} %get-tuple-element.37), channel_id=1, source_target_pairs={{4,0},{8,4},{12,8},{0,12},{5,1},{9,5},{13,9},{1,13},{6,2},{10,6},{... | collective-permute-start | bytes 24584 | tf_op jit(solution)/shard_map/ppermute | solution.py:429
  43.8 4.5 %collective-permute-start.7 = (bf16[8,512]{1,0:T(8,128)(2,1)S(1)}, bf16[8,512]{1,0:T(8,128)(2,1)S(1)}, u32[]{:S(2)}, u32[]{:S(2)}) collective-permute-start(bf16[8,512]{1,0:T(8,128)(2,1)S(1)} %get-tuple-element.38), channel_id=1, source_target_pairs={{8,0},{12,4},{0,8},{4,12},{9,1},{13,5},{1,9},{5,13},{10,2},{14,6},... | collective-permute-start | bytes 24584 | tf_op jit(solution)/shard_map/ppermute | solution.py:429
  44.2 5.8 %collective-permute-start.8 = (bf16[8,512]{1,0:T(8,128)(2,1)S(1)}, bf16[8,512]{1,0:T(8,128)(2,1)S(1)}, u32[]{:S(2)}, u32[]{:S(2)}) collective-permute-start(bf16[8,512]{1,0:T(8,128)(2,1)S(1)} %get-tuple-element.39), channel_id=1, source_target_pairs={{12,0},{0,4},{4,8},{8,12},{13,1},{1,5},{5,9},{9,13},{14,2},{2,6},{... | collective-permute-start | bytes 24584 | tf_op jit(solution)/shard_map/ppermute | solution.py:429
  49.9 2.2 %copy-start.4 = (bf16[512,4096]{1,0:T(8,128)(2,1)S(1)}, bf16[512,4096]{1,0:T(8,128)(2,1)}, u32[]{:S(2)}) copy-start(bf16[512,4096]{1,0:T(8,128)(2,1)} %copy-done.3) | copy-start | bytes 12582916
  54.3 0.8 %copy-start.11 = (f32[64,2048]{1,0:T(8,128)}, f32[64,2048]{1,0:T(8,128)S(1)}, u32[]{:S(2)}) copy-start(f32[64,2048]{1,0:T(8,128)S(1)} %get-tuple-element.43.refs_0_) | copy-start | bytes 1572868
  55.1 0.6 copy-start.18
  55.8 17.9 %copy-start.15 = (bf16[96,2048]{1,0:T(8,128)(2,1)S(1)}, bf16[96,2048]{1,0:T(8,128)(2,1)}, u32[]{:S(2)}) copy-start(bf16[96,2048]{1,0:T(8,128)(2,1)} %copy-done.14) | copy-start | bytes 1179652
  61.2 12.5 %collective-permute-start.9 = (bf16[256,2048]{1,0:T(8,128)(2,1)}, bf16[256,2048]{1,0:T(8,128)(2,1)S(1)}, u32[]{:S(2)}, u32[]{:S(2)}) collective-permute-start(bf16[256,2048]{1,0:T(8,128)(2,1)} %get-tuple-element.42), channel_id=1, source_target_pairs={{0,1},{1,0},{2,3},{3,2},{4,5},{5,4},{6,7},{7,6},{8,9},{9,8},{10,11... | collective-permute-start | bytes 3145736 | tf_op jit(solution)/shard_map/ppermute | solution.py:457
  61.3 2.7 %collective-permute-start.11 = (bf16[64,2048]{1,0:T(8,128)(2,1)S(1)}, bf16[64,2048]{1,0:T(8,128)(2,1)S(1)}, u32[]{:S(2)}, u32[]{:S(2)}) collective-permute-start(bf16[64,2048]{1,0:T(8,128)(2,1)S(1)} %get-tuple-element.44), channel_id=1, source_target_pairs={{0,1},{1,0},{2,3},{3,2},{4,5},{5,4},{6,7},{7,6},{8,9},{9,8},{10,11... | collective-permute-start | bytes 786440 | tf_op jit(solution)/shard_map/ppermute | solution.py:368
  61.8 0.7 copy-start.12
  65.0 8.6 %collective-permute-start.12 = (bf16[64,2048]{1,0:T(8,128)(2,1)S(1)}, bf16[64,2048]{1,0:T(8,128)(2,1)S(1)}, u32[]{:S(2)}, u32[]{:S(2)}) collective-permute-start(bf16[64,2048]{1,0:T(8,128)(2,1)S(1)} %add_convert_fusion.2), channel_id=1, source_target_pairs={{0,2},{1,3},{2,0},{3,1},{4,6},{5,7},{6,4},{7,5},{8,10},{9,11},{10,... | collective-permute-start | bytes 786440 | tf_op jit(solution)/shard_map/ppermute | solution.py:374
  73.7 1.6 %copy-start.10 = (f32[256,2048]{1,0:T(8,128)S(1)}, f32[256,2048]{1,0:T(8,128)}, u32[]{:S(2)}) copy-start(f32[256,2048]{1,0:T(8,128)} %get-tuple-element.41.keep) | copy-start | bytes 6291460
  75.3 1.0 %copy-start.13 = (bf16[96,2048]{1,0:T(8,128)(2,1)S(1)}, bf16[96,2048]{1,0:T(8,128)(2,1)}, u32[]{:S(2)}) copy-start(bf16[96,2048]{1,0:T(8,128)(2,1)} %copy-done.12) | copy-start | bytes 1179652

commit v2 on v1

v2 whole, which is shorter than its diff:
```python
import functools

import jax
import jax.numpy as jnp
from jax import lax
from jax.experimental import pallas as pl
from jax.experimental.pallas import tpu as pltpu
from jax.sharding import PartitionSpec as P

LOG2E = 1.4426950408889634
MASKED = -1e30
GROUP = 6
NEVER = 2**30

VMEM = pl.BlockSpec(memory_space=pltpu.VMEM)
SMEM = pl.BlockSpec(memory_space=pltpu.SMEM)
ANY = pl.BlockSpec(memory_space=pl.ANY)


def attend_group(queries, tokens, contexts, live_lengths, step_count):
    count = len(queries)
    head_dim = tokens[0].shape[1] // 2
    head_count = queries[0].shape[1] // head_dim
    rows = head_count * step_count
    gain = LOG2E / head_dim**0.5
    stacked = jnp.concatenate(
        [
            query[:, h * head_dim : (h + 1) * head_dim]
            for query in queries
            for h in range(head_count)
        ],
        axis=0,
    ).astype(jnp.bfloat16)
    tokens = jnp.concatenate(tokens, axis=0).astype(jnp.bfloat16)
    score_new = contract_last(stacked, tokens[:, :head_dim])
    row_ids = lax.broadcasted_iota(jnp.int32, score_new.shape, 0)
    column_ids = lax.broadcasted_iota(jnp.int32, score_new.shape, 1)
    allowed = (row_ids // rows == column_ids // step_count) & (
        column_ids % step_count <= row_ids % step_count
    )
    score_new = jnp.where(allowed, score_new, MASKED)
    new_max = jnp.max(score_new, axis=1, keepdims=True)
    maxima, scores = [], []
    for g in range(count):
        keys = jnp.concatenate([page[:, :head_dim] for page in contexts[g]], axis=0)
        score = contract_last(stacked[g * rows : (g + 1) * rows], keys)
        position = lax.broadcasted_iota(jnp.int32, score.shape, 1)
        score = jnp.where(position < live_lengths[g], score, MASKED)
        scores.append(score)
        maxima.append(
            jnp.maximum(
                jnp.max(score, axis=1, keepdims=True), new_max[g * rows : (g + 1) * rows]
            )
        )
    exp_new = jnp.exp2((score_new - jnp.concatenate(maxima, axis=0)) * gain)
    new_total = jnp.sum(exp_new, axis=1, keepdims=True)
    results, inverses = [], []
    for g in range(count):
        exp_ctx = jnp.exp2((scores[g] - maxima[g]) * gain)
        total = jnp.sum(exp_ctx, axis=1, keepdims=True) + new_total[g * rows : (g + 1) * rows]
        inverse = 1.0 / total
        inverses.append(inverse)
        values = jnp.concatenate([page[:, head_dim:] for page in contexts[g]], axis=0)
        results.append(
            jnp.dot(
                (exp_ctx * inverse).astype(jnp.bfloat16),
                values,
                preferred_element_type=jnp.float32,
            )
        )
    weight_new = (exp_new * jnp.concatenate(inverses, axis=0)).astype(jnp.bfloat16)
    result = jnp.concatenate(results, axis=0) + jnp.dot(
        weight_new, tokens[:, head_dim:], preferred_element_type=jnp.float32
    )
    return [
        jnp.concatenate(
            [
                result[g * rows + h * step_count : g * rows + (h + 1) * step_count]
                for h in range(head_count)
            ],
            axis=1,
        )
        for g in range(count)
    ]


def contract_last(a, b):
    return lax.dot_general(a, b, (((1,), (1,)), ((), ())), preferred_element_type=jnp.float32)


def route_of(migration, own_index, peer, arriving):
    ours, theirs, slot_row = (2, 0, 3) if arriving else (0, 2, 1)
    slot = jnp.int32(0)
    for row in range(migration.shape[1]):
        match = (migration[ours, row] == own_index) & (migration[theirs, row] == peer)
        slot = jnp.where(match, migration[slot_row, row], slot)
    return slot


def arrivals_of(migration, inst_count):
    me = lax.axis_index("inst")
    incoming = migration.shape[1] // inst_count
    slots = [jnp.int32(NEVER)] * incoming
    sources = [jnp.int32(0)] * incoming
    for row in range(migration.shape[1]):
        slot = jnp.where(migration[2, row] == me, migration[3, row], NEVER)
        source = migration[0, row]
        for i in range(incoming):
            before = slot < slots[i]
            slots[i], slot = jnp.where(before, slot, slots[i]), jnp.where(before, slots[i], slot)
            sources[i], source = (
                jnp.where(before, source, sources[i]),
                jnp.where(before, sources[i], source),
            )
    return slots, sources


def slot_at(position, arrivals, slot_count):
    kept = slot_count - len(arrivals)
    if position >= kept:
        return jnp.minimum(arrivals[position - kept], slot_count - 1)
    slot = jnp.int32(position)
    for arrival in arrivals:
        slot = slot + (slot >= arrival).astype(jnp.int32)
    return slot


def pack_kernel(inst_count, migration, queries, new_tokens, after, *outs):
    me = lax.axis_index("inst")
    width = queries.shape[2]
    for shift, out in enumerate(outs):
        slot = route_of(migration, me, lax.rem(me + shift + 1, inst_count), True)
        out[:, :width] = queries[slot]
        out[:, width:] = new_tokens[slot]


def page_copies(pool, buffer, sems, page_table, item, slot):
    page_count = page_table.shape[0]
    for j in range(page_count):
        pltpu.make_async_copy(
            pool.at[page_table[j, slot]], buffer.at[item, j], sems.at[item]
        ).start()


def wait_copies(pool, buffer, sems, item):
    pltpu.make_async_copy(
        pool.at[pl.ds(0, buffer.shape[1])], buffer.at[item], sems.at[item]
    ).wait()


def away_kernel(inst_count, lengths, page_table, migration, after, *refs):
    count = inst_count - 1
    received, pool, outs = refs[:count], refs[count], refs[count + 1 : 2 * count + 1]
    buffer, sems = refs[2 * count + 1 :]
    page_count, slot_count = page_table.shape
    page_len = pool.shape[1]
    me = lax.axis_index("inst")
    step_count, width = outs[0].shape
    live = []
    for k in range(count):
        peer = lax.rem(me + inst_count - (k + 1), inst_count)
        slot = route_of(migration, me, peer, False)
        page_copies(pool, buffer, sems, page_table, k, slot)
        live.append(lengths[me * slot_count + slot] * page_len)
    for k in range(count):
        wait_copies(pool, buffer, sems, k)
    result = attend_group(
        [ref[:, :width].astype(jnp.float32) for ref in received],
        [ref[:, width:].astype(jnp.float32) for ref in received],
        [[buffer.at[k, j] for j in range(page_count)] for k in range(count)],
        live,
        step_count,
    )
    for k in range(count):
        outs[k][...] = result[k].astype(jnp.bfloat16)


def project(attended, weight, first, columns, target, offset):
    tile = min(512, columns)
    rows = attended[...]
    for j in range(0, columns, tile):
        start = pl.multiple_of(first + j, tile)
        target[:, offset + j : offset + j + tile] = jnp.dot(
            rows, weight[:, pl.ds(start, tile)], preferred_element_type=jnp.float32
        ).astype(target.dtype)


def project_far(attended, far_weight, keep, send):
    core = lax.rem(lax.axis_index("tp"), 2)
    chips = lax.axis_size("tp") // 2
    columns = far_weight.shape[1] // (2 * chips - 2)
    for target, side in ((send, 1 - core), (keep, core)):
        for d in range(chips - 1):
            project(
                attended, far_weight, (2 * d + side) * columns, columns, target, d * columns
            )


def attend_chunk(
    inst_count, first, migration, lengths, page_table, queries, new_tokens, pool, answers,
    attended, buffer, sems,
    between=lambda: None,
):
    page_count, slot_count = page_table.shape
    page_len = pool.shape[1]
    step_count = queries.shape[1]
    count = attended.shape[0] // step_count
    me = lax.axis_index("inst")
    arrivals, sources = arrivals_of(migration, inst_count)
    local = min(count, slot_count - len(arrivals) - first)
    slots = [slot_at(first + i, arrivals, slot_count) for i in range(local)]
    for i, slot in enumerate(slots):
        page_copies(pool, buffer, sems, page_table, i, slot)
    between()
    rows = []
    for base in range(0, local, GROUP):
        items = range(base, min(base + GROUP, local))
        for i in items:
            wait_copies(pool, buffer, sems, i)
        rows += attend_group(
            [queries[slots[i]].astype(jnp.float32) for i in items],
            [new_tokens[slots[i]].astype(jnp.float32) for i in items],
            [[buffer.at[i, j] for j in range(page_count)] for i in items],
            [lengths[me * slot_count + slots[i]] * page_len for i in items],
            step_count,
        )
    for m in range(count - local):
        chosen = lax.rem(sources[m] - me + inst_count, inst_count) - 1
        row = answers[0][...].astype(jnp.float32)
        for k in range(1, len(answers)):
            row = jnp.where(chosen == k, answers[k][...].astype(jnp.float32), row)
        rows.append(row)
    for pair in range(0, count, 2):
        attended[pair * step_count : (pair + 2) * step_count, :] = jnp.concatenate(
            rows[pair : pair + 2], axis=0
        ).astype(jnp.bfloat16)


def first_kernel(
    inst_count, migration, lengths, page_table, queries, new_tokens, pool, weight,
    attended, keep, send, far_weight, buffer, page_sems, weight_sems,
):
    own_tp = lax.axis_index("tp")
    chips = lax.axis_size("tp") // 2
    pair_columns = weight.shape[1] // chips

    def weight_copy(d):
        chip = lax.rem(own_tp // 2 + d, chips)
        start = pl.multiple_of(chip * pair_columns, pair_columns)
        return pltpu.make_async_copy(
            weight.at[:, pl.ds(start, pair_columns)],
            far_weight.at[:, pl.ds((d - 1) * pair_columns, pair_columns)],
            weight_sems.at[d - 1],
        )

    def start_weight():
        for d in range(1, chips):
            weight_copy(d).start()

    attend_chunk(
        inst_count, 0, migration, lengths, page_table, queries, new_tokens, pool, (),
        attended, buffer, page_sems, start_weight,
    )
    for d in range(1, chips):
        weight_copy(d).wait()
    project_far(attended, far_weight, keep, send)


def chunk_kernel(
    inst_count, first, migration, lengths, page_table, queries, new_tokens, pool, far_weight,
    after, *refs
):
    answers, (attended, keep, send, buffer, sems) = refs[:-5], refs[-5:]
    attend_chunk(
        inst_count, first, migration, lengths, page_table, queries, new_tokens, pool, answers,
        attended, buffer, sems,
    )
    project_far(attended, far_weight, keep, send)


def own_kernel(weight, *refs):
    attended, (keep, send, rows, near_weight, sems) = refs[:-5], refs[-5:]
    core = lax.rem(lax.axis_index("tp"), 2)
    chip = lax.axis_index("tp") // 2
    columns = keep.shape[1]
    copies = []
    for n, side in enumerate((1 - core, core)):
        start = pl.multiple_of((chip * 2 + side) * columns, columns)
        copies.append(
            pltpu.make_async_copy(
                weight.at[:, pl.ds(start, columns)], near_weight.at[n], sems.at[n]
            )
        )
        copies[n].start()
    at = 0
    for ref in attended:
        rows[at : at + ref.shape[0], :] = ref[...]
        at += ref.shape[0]
    for n, target in enumerate((send, keep)):
        copies[n].wait()
        project(rows, near_weight.at[n], 0, columns, target, 0)


def sum_kernel(inst_count, chunks, migration, keep, mate, *refs):
    (out, last, staged, sem), parts = refs[-4:], refs[:-4]
    slot_count, step_count, _ = out.shape
    pair = 2 * step_count
    arrivals, _ = arrivals_of(migration, inst_count)
    share = len(parts) // len(chunks)
    at = 0
    for n, chunk in enumerate(chunks):
        for base in range(0, chunk, pair):
            total = keep[at : at + pair, :] + mate[at : at + pair, :].astype(jnp.float32)
            for part in parts[n * share : (n + 1) * share]:
                total = total + part[base : base + pair, :].astype(jnp.float32)
            total = total.astype(jnp.bfloat16)
            for half in range(2):
                staged[at // step_count + half] = total[half * step_count : (half + 1) * step_count]
            at += pair
    scatter_rows(staged, out, arrivals, 0, sem)
    last[...] = keep[at:, :] + mate[at:, :].astype(jnp.float32)


def scatter_rows(staged, out, arrivals, first, sem):
    slot_count = out.shape[0]
    for i in range(staged.shape[0]):
        slot = slot_at(first + i, arrivals, slot_count)
        pltpu.make_async_copy(staged.at[i], out.at[slot], sem.at[0]).start()
    pltpu.make_async_copy(staged, out.at[pl.ds(0, staged.shape[0])], sem.at[0]).wait()


def last_kernel(inst_count, first, migration, last, *refs):
    parts, (out, staged, sem) = refs[:-4], refs[-3:]
    step_count = out.shape[1]
    pair = 2 * step_count
    arrivals, _ = arrivals_of(migration, inst_count)
    for at in range(0, last.shape[0], pair):
        total = last[at : at + pair, :]
        for part in parts:
            total = total + part[at : at + pair, :].astype(jnp.float32)
        total = total.astype(jnp.bfloat16)
        for half in range(2):
            staged[at // step_count + half] = total[half * step_count : (half + 1) * step_count]
    scatter_rows(staged, out, arrivals, first, sem)


def chunk_sizes(slot_count):
    large = (slot_count * 3 // 16) * 2
    return [large, large, slot_count - 2 * large]


def in_hbm(value):
    return pltpu.with_memory_space_constraint(value, pltpu.HBM)


def in_vmem(value):
    return pltpu.with_memory_space_constraint(value, pltpu.VMEM)


def on_device(queries, new_kv, kv_pool, out_weight, lengths, page_table, migration):
    inst_count = lax.axis_size("inst")
    tp_count = lax.axis_size("tp")
    chips = tp_count // 2
    slot_count, page_count = page_table.shape
    row_count, width = queries.shape
    step_count = row_count // slot_count
    queries = in_hbm(queries.reshape(slot_count, step_count, width))
    new_tokens = in_hbm(new_kv[0].reshape(slot_count, step_count, new_kv.shape[2]))
    pool = in_hbm(kv_pool[0])
    page_shape = pool.shape[1:]
    columns = out_weight.shape[1] // tp_count
    weight = in_hbm(out_weight)
    lengths = in_hbm(lengths)
    page_table = in_hbm(page_table.T)
    migration = in_hbm(migration.T)
    others = inst_count - 1
    limit = pltpu.CompilerParams(vmem_limit_bytes=32 * 2**20)
    light = pl.CostEstimate(flops=1, bytes_accessed=1, transcendentals=0)
    bf16, f32 = jnp.bfloat16, jnp.float32
    shape = jax.ShapeDtypeStruct
    swap = [(t, t ^ 1) for t in range(tp_count)]
    forward = [[(i, (i + k) % inst_count) for i in range(inst_count)] for k in range(inst_count)]
    far = (chips - 1) * columns
    arrived = []

    def hold(value, until):
        return pl.pallas_call(
            lambda *refs: None,
            out_shape=shape(value.shape, value.dtype),
            in_specs=[ANY] * (1 + len(until)),
            out_specs=ANY,
            input_output_aliases={0: 0},
            cost_estimate=light,
            name="hold",
        )(value, *until)

    def exchange(keep, send, gate=()):
        mate = lax.ppermute(send, "tp", swap)
        if arrived:
            keep = hold(keep, [*arrived[-(chips - 1) :], *gate])
        summed = (keep + mate.astype(f32)).astype(bf16)
        for d in range(1, chips):
            arrived.append(
                lax.ppermute(
                    summed[:, (d - 1) * columns : d * columns],
                    "tp",
                    [(t, (t + 2 * d) % tp_count) for t in range(tp_count)],
                )
            )
        return summed

    def chunk_shapes(count):
        rows = count * step_count
        return [
            pltpu.VMEM((rows, width), bf16),
            pltpu.VMEM((rows, far), f32),
            pltpu.VMEM((rows, far), bf16),
        ]

    def page_scratch(count):
        return [
            pltpu.VMEM((count, page_count, *page_shape), bf16),
            pltpu.SemaphoreType.DMA((count,)),
        ]

    counts = chunk_sizes(slot_count)
    attended, keep, send, far_weight = pl.pallas_call(
        functools.partial(first_kernel, inst_count),
        out_shape=chunk_shapes(counts[0]) + [pltpu.VMEM((width, 2 * far), bf16)],
        in_specs=[SMEM, SMEM, SMEM, VMEM, VMEM, ANY, ANY],
        out_specs=[VMEM] * 4,
        scratch_shapes=page_scratch(counts[0]) + [pltpu.SemaphoreType.DMA((chips - 1,))],
        compiler_params=limit,
        cost_estimate=light,
        name="attend_first",
    )(migration, lengths, page_table, queries, new_tokens, pool, weight)
    chunks = [attended]
    after = exchange(keep, send)
    packs = pl.pallas_call(
        functools.partial(pack_kernel, inst_count),
        out_shape=[shape((step_count, width + new_tokens.shape[2]), bf16)] * others,
        in_specs=[SMEM, VMEM, VMEM, ANY],
        out_specs=[VMEM] * others,
        compiler_params=limit,
        cost_estimate=light,
        name="pack",
    )(migration, queries, new_tokens, after)
    received = [lax.ppermute(packs[k - 1], "inst", forward[k]) for k in range(1, inst_count)]
    first = counts[0]
    after = packs[0]
    answers = []
    for count in counts[1:]:
        given = answers if first + count == slot_count else []
        attended, keep, send = pl.pallas_call(
            functools.partial(chunk_kernel, inst_count, first),
            out_shape=chunk_shapes(count),
            in_specs=[SMEM, SMEM, SMEM, VMEM, VMEM, ANY, VMEM, ANY] + [VMEM] * len(given),
            out_specs=[VMEM] * 3,
            scratch_shapes=page_scratch(count),
            compiler_params=limit,
            cost_estimate=light,
            name="attend_chunk",
        )(
            migration, lengths, page_table, queries, new_tokens, pool, in_vmem(far_weight),
            after, *given,
        )
        chunks.append(attended)
        gate = []
        if first + count == slot_count - counts[-1]:
            answers = pl.pallas_call(
                functools.partial(away_kernel, inst_count),
                out_shape=[shape((step_count, width), bf16)] * others,
                in_specs=[SMEM, SMEM, SMEM, ANY] + [VMEM] * others + [ANY],
                out_specs=[VMEM] * others,
                scratch_shapes=page_scratch(others),
                compiler_params=limit,
                cost_estimate=light,
                name="attend_away",
            )(lengths, page_table, migration, chunks[-1], *received, pool)
            gate = answers[:1]
            answers = [
                lax.ppermute(answers[k - 1], "inst", [(b, a) for a, b in forward[k]])
                for k in range(1, inst_count)
            ]
        after = exchange(keep, send, gate)
        first += count
    keep, send = pl.pallas_call(
        own_kernel,
        out_shape=[pltpu.VMEM((row_count, columns), f32), pltpu.VMEM((row_count, columns), bf16)],
        in_specs=[ANY] + [VMEM] * len(counts),
        out_specs=[VMEM] * 2,
        scratch_shapes=[
            pltpu.VMEM((row_count, width), bf16),
            pltpu.VMEM((2, width, columns), bf16),
            pltpu.SemaphoreType.DMA((2,)),
        ],
        compiler_params=limit,
        cost_estimate=light,
        name="own_columns",
    )(weight, *[in_vmem(chunk) for chunk in chunks])
    mate = lax.ppermute(send, "tp", swap)
    early = slot_count - counts[-1]
    out_shape = (slot_count, step_count, columns)
    out, last = pl.pallas_call(
        functools.partial(
            sum_kernel, inst_count, [count * step_count for count in counts[:-1]]
        ),
        out_shape=[pltpu.HBM(out_shape, bf16), pltpu.VMEM((counts[-1] * step_count, columns), f32)],
        in_specs=[SMEM] + [VMEM] * (2 + len(arrived) - chips + 1),
        out_specs=[ANY, VMEM],
        scratch_shapes=[
            pltpu.VMEM((early, step_count, columns), bf16),
            pltpu.SemaphoreType.DMA((1,)),
        ],
        compiler_params=limit,
        cost_estimate=light,
        name="sum_early",
    )(migration, in_vmem(keep), mate, *arrived[: 1 - chips])
    out = pl.pallas_call(
        functools.partial(last_kernel, inst_count, early),
        out_shape=pltpu.HBM(out_shape, bf16),
        in_specs=[SMEM] + [VMEM] * chips + [ANY],
        out_specs=ANY,
        scratch_shapes=[
            pltpu.VMEM((counts[-1], step_count, columns), bf16),
            pltpu.SemaphoreType.DMA((1,)),
        ],
        input_output_aliases={1 + chips: 0},
        compiler_params=limit,
        cost_estimate=light,
        name="sum_last",
    )(migration, in_vmem(last), *arrived[1 - chips :], out)
    return out.reshape(row_count, columns)


def solution(mesh):
    placed = (
        P(("group", "inst"), "tp"),
        P("tp", ("group", "inst"), None),
        P("tp", ("group", "inst"), None, None),
        P("tp", None),
        P("group"),
        P(("group", "inst"), None),
        P("group", None),
    )
    return jax.shard_map(
        on_device, mesh=mesh, in_specs=placed, out_specs=P(("group", "inst"), "tp"), check_vma=False
    )
```

time: 78.6 us -> 62.4 us (0.79)
  local copies, waits for them, and re-layouts: 19.8 us -> 6.12 us
  waiting for transfers between devices: 22 us -> 13 us
  Pallas kernels: 20.8 us -> 25.4 us
  starting transfers between devices: 13.1 us -> 14.8 us
    unnamed x50 -> x18, local copies, waits for them, and re-layouts: 19.8 us -> 6.12 us
    ppermute x3, waiting for transfers between devices: 10.3 us -> 3.64 us  [exchange(): lax.ppermute(summed[:, (d - 1) * columns:d * columns], 'tp', [(t, (t + 2...]
    pallas_call x4 -> x5, Pallas kernels: 12.5 us -> 16.3 us  [the longest x2 9.15 us: on_device(): pl.pallas_call(functools.partial(chunk_kernel, inst_count, first), out_sh...]
    ppermute x3, waiting for transfers between devices: 4.07 us -> 1.63 us  [on_device(): lax.ppermute(answers[k - 1], 'inst', [(b, a) for a, b in forward[k]])]
    ppermute x3, starting transfers between devices: 2.03 us -> 3.83 us  [on_device(): lax.ppermute(answers[k - 1], 'inst', [(b, a) for a, b in forward[k]])]
    pallas_call x1, Pallas kernels: 1.31 us -> 2.64 us  [on_device(): pl.pallas_call(functools.partial(away_kernel, inst_count), out_shape=[sha...]
    pallas_call x1, Pallas kernels: 6.31 us -> 5.32 us  [on_device(): pl.pallas_call(functools.partial(first_kernel, inst_count), out_shape=chu...]
  transfers between devices with their start and end apart: 13 -> 13, of which waited for: 9 -> 7; matrix products, arithmetic and copies ran while one was open for 1% -> 2% of each run, Pallas kernels for 15% -> 28%
where the time goes in v2:
time: 62.4 us; the launch traced here: 61.8 us
  Pallas kernels  25.4 us (41%)
  starting transfers between devices  14.8 us (24%)
  waiting for transfers between devices  13 us (21%)
  local copies, waits for them, and re-layouts  6.12 us (10%)
  other arithmetic  2.45 us (4%)
    pallas_call x2, Pallas kernels, on_device(): pl.pallas_call(functools.partial(chunk_kernel, inst_count, first), out_sh...  9.15 us
    unnamed x18, local copies, waits for them, and re-layouts  6.12 us
    pallas_call x1, Pallas kernels, on_device(): pl.pallas_call(functools.partial(first_kernel, inst_count), out_shape=chu...  5.32 us
    ppermute x3, starting transfers between devices, exchange(): lax.ppermute(summed[:, (d - 1) * columns:d * columns], 'tp', [(t, (t + 2...  5.11 us
    ppermute x3, waiting for transfers between devices, on_device(): lax.ppermute(packs[k - 1], 'inst', forward[k])  4.81 us
    ppermute x3, starting transfers between devices, on_device(): lax.ppermute(packs[k - 1], 'inst', forward[k])  4.68 us
    ppermute x3, starting transfers between devices, on_device(): lax.ppermute(answers[k - 1], 'inst', [(b, a) for a, b in forward[k]])  3.83 us
    ppermute x3, waiting for transfers between devices, exchange(): lax.ppermute(summed[:, (d - 1) * columns:d * columns], 'tp', [(t, (t + 2...  3.64 us
  transfers between devices with their start and end apart: 13, of which 7 were waited for; matrix products, arithmetic and copies ran while one was open for 2% of the time, Pallas kernels for 28%

profile of v2, /device:TPU:0, one launch (start us, length us, event | category | flops | bytes accessed | tf_op | source)
XLA Modules:
  0.0 61.8 jit_solution(5221073445832536747)
XLA Ops:
  0.0 5.3 %attend_first.1 = (bf16[96,512]{1,0:T(8,128)(2,1)S(1)}, f32[96,2048]{1,0:T(8,128)S(1)}, bf16[96,2048]{1,0:T(8,128)(2,1)S(1)}, bf16[512,4096]{1,0:T(8,128)(2,1)S(1)}) custom-call(s32[4,12]{1,0:T(4,128)} %bitcast.18, s32[128]{0:T(128)} %lengths.7, s32[4,32]{1,0:T(4,128)} %bitcast.25, bf16[32,8,512]{2,1,0:T(8,128)(2,1)} %bitcast.10, ...), custom_call_target="tpu_custom_call" | custom-call | flops 1 | bytes 1 | tf_op jit(solution)/shard_map/attend_first/pallas_call | solution.py:427
  5.3 0.0 copy-start
  5.3 0.5 collective-permute-start
  5.9 1.3 %collective-permute-done = bf16[96,2048]{1,0:T(8,128)(2,1)S(1)} collective-permute-done((bf16[96,2048]{1,0:T(8,128)(2,1)S(1)}, bf16[96,2048]{1,0:T(8,128)(2,1)S(1)}, u32[]{:S(2)}, u32[]{:S(2)}) %collective-permute-start) | collective-permute-done | bytes 393248 | tf_op jit(solution)/shard_map/ppermute | solution.py:398
  7.2 0.1 add_convert_fusion.1.after
  7.3 1.1 %pack.1 = (bf16[8,768]{1,0:T(8,128)(2,1)S(1)}, bf16[8,768]{1,0:T(8,128)(2,1)S(1)}, bf16[8,768]{1,0:T(8,128)(2,1)S(1)}) custom-call(s32[4,12]{1,0:T(4,128)} %bitcast.19, bf16[32,8,512]{2,1,0:T(8,128)(2,1)} %bitcast.11, bf16[32,8,256]{2,1,0:T(8,128)(2,1)} %bitcast.15, bf16[96,2048]{1,0:T(8,128)(2,1)S(1)} %add_convert_fusion.1.after), custom_call_target="tpu_custom_call" | custom-call | flops 1 | bytes 1 | tf_op jit(solution)/shard_map/pack/pallas_call | solution.py:439
  8.4 3.0 %collective-permute-start.1 = (bf16[96,2048]{1,0:T(8,128)(2,1)S(1)}, bf16[96,2048]{1,0:T(8,128)(2,1)S(1)}, u32[]{:S(2)}, u32[]{:S(2)}) collective-permute-start(bf16[96,2048]{1,0:T(8,128)(2,1)S(1)} %add_convert_fusion.1.after), channel_id=1, source_target_pairs={{0,2},{1,3},{2,0},{3,1},{4,6},{5,7},{6,4},{7,5},{8,10},{9,11},{10,... | collective-permute-start | bytes 1179656 | tf_op jit(solution)/shard_map/ppermute | solution.py:404
  11.4 5.0 %attend_chunk.2 = (bf16[96,512]{1,0:T(8,128)(2,1)S(1)}, f32[96,2048]{1,0:T(8,128)S(1)}, bf16[96,2048]{1,0:T(8,128)(2,1)S(1)}) custom-call(s32[4,12]{1,0:T(4,128)} %bitcast.20, s32[128]{0:T(128)} %lengths.7, s32[4,32]{1,0:T(4,128)} %bitcast.26, bf16[32,8,512]{2,1,0:T(8,128)(2,1)} %bitcast.12, bf16[32,8,256]{2,1,0:T(8,128)(2,1)} %bitcast.16, ...), custom_call_target="tpu_custom_call" | custom-call | flops 1 | bytes 1 | tf_op jit(solution)/shard_map/attend_chunk/pallas_call | solution.py:454
  16.4 0.0 copy-start.2
  16.4 0.1 collective-permute-start.5
  16.5 2.7 %collective-permute-start.3 = (bf16[8,768]{1,0:T(8,128)(2,1)S(1)}, bf16[8,768]{1,0:T(8,128)(2,1)S(1)}, u32[]{:S(2)}, u32[]{:S(2)}) collective-permute-start(bf16[8,768]{1,0:T(8,128)(2,1)S(1)} %get-tuple-element.32), channel_id=1, source_target_pairs={{0,8},{4,12},{8,0},{12,4},{1,9},{5,13},{9,1},{13,5},{2,10},{6,14},... | collective-permute-start | bytes 36872 | tf_op jit(solution)/shard_map/ppermute | solution.py:448
  19.2 1.3 %collective-permute-start.4 = (bf16[8,768]{1,0:T(8,128)(2,1)S(1)}, bf16[8,768]{1,0:T(8,128)(2,1)S(1)}, u32[]{:S(2)}, u32[]{:S(2)}) collective-permute-start(bf16[8,768]{1,0:T(8,128)(2,1)S(1)} %get-tuple-element.33), channel_id=1, source_target_pairs={{0,12},{4,0},{8,4},{12,8},{1,13},{5,1},{9,5},{13,9},{2,14},{6,2},{... | collective-permute-start | bytes 36872 | tf_op jit(solution)/shard_map/ppermute | solution.py:448
  20.5 0.7 %collective-permute-start.2 = (bf16[8,768]{1,0:T(8,128)(2,1)S(1)}, bf16[8,768]{1,0:T(8,128)(2,1)S(1)}, u32[]{:S(2)}, u32[]{:S(2)}) collective-permute-start(bf16[8,768]{1,0:T(8,128)(2,1)S(1)} %get-tuple-element.29.after), channel_id=1, source_target_pairs={{0,4},{4,8},{8,12},{12,0},{1,5},{5,9},{9,13},{13,1},{2,6},{6,10},{... | collective-permute-start | bytes 36872 | tf_op jit(solution)/shard_map/ppermute | solution.py:448
  21.2 0.0 collective-permute-done.3.refs_1_
  21.2 1.7 %collective-permute-done.4.refs_2_ = bf16[8,768]{1,0:T(8,128)(2,1)S(1)} collective-permute-done((bf16[8,768]{1,0:T(8,128)(2,1)S(1)}, bf16[8,768]{1,0:T(8,128)(2,1)S(1)}, u32[]{:S(2)}, u32[]{:S(2)}) %collective-permute-start.4) | collective-permute-done | bytes 12320 | tf_op jit(solution)/shard_map/ppermute | solution.py:448
  22.8 3.1 %collective-permute-done.2.refs_0_ = bf16[8,768]{1,0:T(8,128)(2,1)S(1)} collective-permute-done((bf16[8,768]{1,0:T(8,128)(2,1)S(1)}, bf16[8,768]{1,0:T(8,128)(2,1)S(1)}, u32[]{:S(2)}, u32[]{:S(2)}) %collective-permute-start.2) | collective-permute-done | bytes 12320 | tf_op jit(solution)/shard_map/ppermute | solution.py:448
  26.0 2.6 %attend_away.1 = (bf16[8,512]{1,0:T(8,128)(2,1)S(1)}, bf16[8,512]{1,0:T(8,128)(2,1)S(1)}, bf16[8,512]{1,0:T(8,128)(2,1)S(1)}) custom-call(s32[128]{0:T(128)} %lengths.7, s32[4,32]{1,0:T(4,128)} %bitcast.27, s32[4,12]{1,0:T(4,128)} %bitcast.21, bf16[96,512]{1,0:T(8,128)(2,1)S(1)} %get-tuple-element.30.after.refs_1_, ...), custom_call_target="tpu_custom_call" | custom-call | flops 1 | bytes 1 | tf_op jit(solution)/shard_map/attend_away/pallas_call | solution.py:470
  28.6 0.0 copy-done
  28.6 0.0 copy-start.8
  28.7 0.6 copy-done.8
  29.2 0.0 collective-permute-done.1.refs_1_.refs_0_
  29.3 0.8 %copy-done.6 = bf16[96,2048]{1,0:T(8,128)(2,1)} copy-done((bf16[96,2048]{1,0:T(8,128)(2,1)}, bf16[96,2048]{1,0:T(8,128)(2,1)S(1)}, u32[]{:S(2)}) %copy-start.6) | copy-done | bytes 393240
  30.0 0.0 collective-permute-done.5
  30.0 1.2 %add_convert_fusion.after = bf16[96,2048]{1,0:T(8,128)(2,1)S(1)} fusion(f32[96,2048]{1,0:T(8,128)} %hold.2, bf16[96,2048]{1,0:T(8,128)(2,1)S(1)} %collective-permute-done.5), kind=kLoop, calls=%fused_computation | loop fusion | flops 589824 | bytes 1572864 | tf_op jit(solution)/shard_map/convert_element_type | solution.py:401
  31.2 0.6 collective-permute-start.10
  31.8 0.0 collective-permute-start.7
  31.8 0.6 collective-permute-start.8
  32.4 3.3 %collective-permute-start.6 = (bf16[8,512]{1,0:T(8,128)(2,1)}, bf16[8,512]{1,0:T(8,128)(2,1)S(1)}, u32[]{:S(2)}, u32[]{:S(2)}) collective-permute-start(bf16[8,512]{1,0:T(8,128)(2,1)} %copy-done.8), channel_id=1, source_target_pairs={{4,0},{8,4},{12,8},{0,12},{5,1},{9,5},{13,9},{1,13},{6,2},{10,6},{... | collective-permute-start | bytes 24584 | tf_op jit(solution)/shard_map/ppermute | solution.py:482
  35.6 0.7 %collective-permute-done.7.refs_1_ = bf16[8,512]{1,0:T(8,128)(2,1)S(1)} collective-permute-done((bf16[8,512]{1,0:T(8,128)(2,1)S(1)}, bf16[8,512]{1,0:T(8,128)(2,1)S(1)}, u32[]{:S(2)}, u32[]{:S(2)}) %collective-permute-start.7) | collective-permute-done | bytes 8224 | tf_op jit(solution)/shard_map/ppermute | solution.py:482
  36.4 0.9 %collective-permute-done.8.refs_2_ = bf16[8,512]{1,0:T(8,128)(2,1)S(1)} collective-permute-done((bf16[8,512]{1,0:T(8,128)(2,1)S(1)}, bf16[8,512]{1,0:T(8,128)(2,1)S(1)}, u32[]{:S(2)}, u32[]{:S(2)}) %collective-permute-start.8) | collective-permute-done | bytes 8224 | tf_op jit(solution)/shard_map/ppermute | solution.py:482
  37.3 0.0 collective-permute-done.6.refs_0_
  37.3 2.2 %copy-done.1 = bf16[512,4096]{1,0:T(8,128)(2,1)S(1)} copy-done((bf16[512,4096]{1,0:T(8,128)(2,1)S(1)}, bf16[512,4096]{1,0:T(8,128)(2,1)}, u32[]{:S(2)}) %copy-start.1) | copy-done | bytes 4194328
  39.5 4.1 %attend_chunk.3 = (bf16[64,512]{1,0:T(8,128)(2,1)S(1)}, f32[64,2048]{1,0:T(8,128)S(1)}, bf16[64,2048]{1,0:T(8,128)(2,1)S(1)}) custom-call(s32[4,12]{1,0:T(4,128)} %bitcast.22, s32[128]{0:T(128)} %lengths.7, s32[4,32]{1,0:T(4,128)} %bitcast.28, bf16[32,8,512]{2,1,0:T(8,128)(2,1)} %bitcast.13, bf16[32,8,256]{2,1,0:T(8,128)(2,1)} %bitcast.17, ...), custom_call_target="tpu_custom_call" | custom-call | flops 1 | bytes 1 | tf_op jit(solution)/shard_map/attend_chunk/pallas_call | solution.py:454
  43.6 0.8 %copy-done.3 = f32[64,2048]{1,0:T(8,128)} copy-done((f32[64,2048]{1,0:T(8,128)}, f32[64,2048]{1,0:T(8,128)S(1)}, u32[]{:S(2)}) %copy-start.3) | copy-done | bytes 524312
  44.4 3.4 %own_columns.1 = (f32[256,2048]{1,0:T(8,128)S(1)}, bf16[256,2048]{1,0:T(8,128)(2,1)}) custom-call(bf16[512,8192]{1,0:T(8,128)(2,1)} %weight.3, bf16[96,512]{1,0:T(8,128)(2,1)S(1)} %get-tuple-element.25.refs_0_, bf16[96,512]{1,0:T(8,128)(2,1)S(1)} %get-tuple-element.30.after.refs_1_, bf16[64,512]{1,0:T(8,128)(2,1)S(1)} %get-tuple-element.38.refs_2_), custom_call_target="tpu_custom_call" | custom-call | flops 1 | bytes 1 | tf_op jit(solution)/shard_map/own_columns/pallas_call | solution.py:487
  47.7 0.1 collective-permute-start.9
  47.8 0.5 collective-permute-start.11
  48.3 0.0 collective-permute-done.10.refs_1_
  48.3 0.8 %copy-done.4 = bf16[96,2048]{1,0:T(8,128)(2,1)} copy-done((bf16[96,2048]{1,0:T(8,128)(2,1)}, bf16[96,2048]{1,0:T(8,128)(2,1)S(1)}, u32[]{:S(2)}) %copy-start.4) | copy-done | bytes 393240
  49.1 1.5 %collective-permute-done.11 = bf16[64,2048]{1,0:T(8,128)(2,1)} collective-permute-done((bf16[64,2048]{1,0:T(8,128)(2,1)S(1)}, bf16[64,2048]{1,0:T(8,128)(2,1)}, u32[]{:S(2)}, u32[]{:S(2)}) %collective-permute-start.11) | collective-permute-done | bytes 262176 | tf_op jit(solution)/shard_map/ppermute | solution.py:398
  50.6 1.2 %add_convert_fusion.2 = bf16[64,2048]{1,0:T(8,128)(2,1)S(1)} fusion(f32[64,2048]{1,0:T(8,128)} %hold.3, bf16[64,2048]{1,0:T(8,128)(2,1)} %collective-permute-done.11), kind=kLoop, calls=%fused_computation.2 | loop fusion | flops 393216 | bytes 1048576 | tf_op jit(solution)/shard_map/convert_element_type | solution.py:401
  51.8 1.6 %collective-permute-start.12 = (bf16[64,2048]{1,0:T(8,128)(2,1)S(1)}, bf16[64,2048]{1,0:T(8,128)(2,1)S(1)}, u32[]{:S(2)}, u32[]{:S(2)}) collective-permute-start(bf16[64,2048]{1,0:T(8,128)(2,1)S(1)} %add_convert_fusion.2), channel_id=1, source_target_pairs={{0,2},{1,3},{2,0},{3,1},{4,6},{5,7},{6,4},{7,5},{8,10},{9,11},{10,... | collective-permute-start | bytes 786440 | tf_op jit(solution)/shard_map/ppermute | solution.py:404
  53.4 0.0 collective-permute-done.9.mate
  53.4 0.0 copy-done.7
  53.4 1.0 %copy-done.5 = bf16[96,2048]{1,0:T(8,128)(2,1)S(1)} copy-done((bf16[96,2048]{1,0:T(8,128)(2,1)S(1)}, bf16[96,2048]{1,0:T(8,128)(2,1)}, u32[]{:S(2)}) %copy-start.5) | copy-done | bytes 393240
  54.4 2.4 %sum_early.1 = (bf16[32,8,2048]{2,1,0:T(8,128)(2,1)}, f32[64,2048]{1,0:T(8,128)S(1)}) custom-call(s32[4,12]{1,0:T(4,128)} %bitcast.23, f32[256,2048]{1,0:T(8,128)S(1)} %get-tuple-element.39.keep, bf16[256,2048]{1,0:T(8,128)(2,1)} %collective-permute-done.9.mate, bf16[96,2048]{1,0:T(8,128)(2,1)S(1)} %copy-done.7, bf16[96,2048]{1,0:T(8,128)(2,1)S(1)} %copy-done.5), custom_call_target="tpu_custom_call" | custom-call | flops 1 | bytes 1 | tf_op jit(solution)/shard_map/sum_early/pallas_call | solution.py:504
  56.8 3.6 %collective-permute-done.12.refs_0_ = bf16[64,2048]{1,0:T(8,128)(2,1)S(1)} collective-permute-done((bf16[64,2048]{1,0:T(8,128)(2,1)S(1)}, bf16[64,2048]{1,0:T(8,128)(2,1)S(1)}, u32[]{:S(2)}, u32[]{:S(2)}) %collective-permute-start.12) | collective-permute-done | bytes 262176 | tf_op jit(solution)/shard_map/ppermute | solution.py:404
  60.4 1.4 %sum_last.1 = bf16[32,8,2048]{2,1,0:T(8,128)(2,1)} custom-call(s32[4,12]{1,0:T(4,128)} %bitcast.24, f32[64,2048]{1,0:T(8,128)S(1)} %get-tuple-element.41.last, bf16[64,2048]{1,0:T(8,128)(2,1)S(1)} %collective-permute-done.12.refs_0_, bf16[32,8,2048]{2,1,0:T(8,128)(2,1)} %get-tuple-element.44.refs_1_), custom_call_target="tpu_custom_call", output_to_operand_aliasing={{}: (3, {})} | custom-call | flops 1 | bytes 1 | tf_op jit(solution)/shard_map/sum_last/pallas_call | solution.py:519
  (9 shorter events, 0.0 us)
Async XLA Ops:
  5.3 23.3 %copy-start = (bf16[512,4096]{1,0:T(8,128)(2,1)}, bf16[512,4096]{1,0:T(8,128)(2,1)S(1)}, u32[]{:S(2)}) copy-start(bf16[512,4096]{1,0:T(8,128)(2,1)S(1)} %get-tuple-element.26.far_weight) | copy-start | bytes 12582916
  5.3 1.9 %collective-permute-start = (bf16[96,2048]{1,0:T(8,128)(2,1)S(1)}, bf16[96,2048]{1,0:T(8,128)(2,1)S(1)}, u32[]{:S(2)}, u32[]{:S(2)}) collective-permute-start(bf16[96,2048]{1,0:T(8,128)(2,1)S(1)} %get-tuple-element.28), channel_id=1, source_target_pairs={{0,1},{1,0},{2,3},{3,2},{4,5},{5,4},{6,7},{7,6},{8,9},{9,8},{10,11... | collective-permute-start | bytes 1179656 | tf_op jit(solution)/shard_map/ppermute | solution.py:398
  8.4 20.9 %collective-permute-start.1 = (bf16[96,2048]{1,0:T(8,128)(2,1)S(1)}, bf16[96,2048]{1,0:T(8,128)(2,1)S(1)}, u32[]{:S(2)}, u32[]{:S(2)}) collective-permute-start(bf16[96,2048]{1,0:T(8,128)(2,1)S(1)} %add_convert_fusion.1.after), channel_id=1, source_target_pairs={{0,2},{1,3},{2,0},{3,1},{4,6},{5,7},{6,4},{7,5},{8,10},{9,11},{10,... | collective-permute-start | bytes 1179656 | tf_op jit(solution)/shard_map/ppermute | solution.py:404
  16.4 12.8 %copy-start.2 = (f32[96,2048]{1,0:T(8,128)}, f32[96,2048]{1,0:T(8,128)S(1)}, u32[]{:S(2)}) copy-start(f32[96,2048]{1,0:T(8,128)S(1)} %get-tuple-element.31.refs_0_) | copy-start | bytes 2359300
  16.4 13.6 %collective-permute-start.5 = (bf16[96,2048]{1,0:T(8,128)(2,1)S(1)}, bf16[96,2048]{1,0:T(8,128)(2,1)S(1)}, u32[]{:S(2)}, u32[]{:S(2)}) collective-permute-start(bf16[96,2048]{1,0:T(8,128)(2,1)S(1)} %get-tuple-element.35), channel_id=1, source_target_pairs={{0,1},{1,0},{2,3},{3,2},{4,5},{5,4},{6,7},{7,6},{8,9},{9,8},{10,11... | collective-permute-start | bytes 1179656 | tf_op jit(solution)/shard_map/ppermute | solution.py:398
  16.5 4.7 %collective-permute-start.3 = (bf16[8,768]{1,0:T(8,128)(2,1)S(1)}, bf16[8,768]{1,0:T(8,128)(2,1)S(1)}, u32[]{:S(2)}, u32[]{:S(2)}) collective-permute-start(bf16[8,768]{1,0:T(8,128)(2,1)S(1)} %get-tuple-element.32), channel_id=1, source_target_pairs={{0,8},{4,12},{8,0},{12,4},{1,9},{5,13},{9,1},{13,5},{2,10},{6,14},... | collective-permute-start | bytes 36872 | tf_op jit(solution)/shard_map/ppermute | solution.py:448
  19.2 3.7 %collective-permute-start.4 = (bf16[8,768]{1,0:T(8,128)(2,1)S(1)}, bf16[8,768]{1,0:T(8,128)(2,1)S(1)}, u32[]{:S(2)}, u32[]{:S(2)}) collective-permute-start(bf16[8,768]{1,0:T(8,128)(2,1)S(1)} %get-tuple-element.33), channel_id=1, source_target_pairs={{0,12},{4,0},{8,4},{12,8},{1,13},{5,1},{9,5},{13,9},{2,14},{6,2},{... | collective-permute-start | bytes 36872 | tf_op jit(solution)/shard_map/ppermute | solution.py:448
  20.5 5.5 %collective-permute-start.2 = (bf16[8,768]{1,0:T(8,128)(2,1)S(1)}, bf16[8,768]{1,0:T(8,128)(2,1)S(1)}, u32[]{:S(2)}, u32[]{:S(2)}) collective-permute-start(bf16[8,768]{1,0:T(8,128)(2,1)S(1)} %get-tuple-element.29.after), channel_id=1, source_target_pairs={{0,4},{4,8},{8,12},{12,0},{1,5},{5,9},{9,13},{13,1},{2,6},{6,10},{... | collective-permute-start | bytes 36872 | tf_op jit(solution)/shard_map/ppermute | solution.py:448
  28.6 0.6 copy-start.8
  29.3 0.8 %copy-start.6 = (bf16[96,2048]{1,0:T(8,128)(2,1)}, bf16[96,2048]{1,0:T(8,128)(2,1)S(1)}, u32[]{:S(2)}) copy-start(bf16[96,2048]{1,0:T(8,128)(2,1)S(1)} %collective-permute-done.1.refs_1_.refs_0_) | copy-start | bytes 1179652
  31.2 17.1 %collective-permute-start.10 = (bf16[96,2048]{1,0:T(8,128)(2,1)S(1)}, bf16[96,2048]{1,0:T(8,128)(2,1)S(1)}, u32[]{:S(2)}, u32[]{:S(2)}) collective-permute-start(bf16[96,2048]{1,0:T(8,128)(2,1)S(1)} %add_convert_fusion.after), channel_id=1, source_target_pairs={{0,2},{1,3},{2,0},{3,1},{4,6},{5,7},{6,4},{7,5},{8,10},{9,11},{10,... | collective-permute-start | bytes 1179656 | tf_op jit(solution)/shard_map/ppermute | solution.py:404
  31.8 4.5 %collective-permute-start.7 = (bf16[8,512]{1,0:T(8,128)(2,1)S(1)}, bf16[8,512]{1,0:T(8,128)(2,1)S(1)}, u32[]{:S(2)}, u32[]{:S(2)}) collective-permute-start(bf16[8,512]{1,0:T(8,128)(2,1)S(1)} %get-tuple-element.36), channel_id=1, source_target_pairs={{8,0},{12,4},{0,8},{4,12},{9,1},{13,5},{1,9},{5,13},{10,2},{14,6},... | collective-permute-start | bytes 24584 | tf_op jit(solution)/shard_map/ppermute | solution.py:482
  31.8 5.4 %collective-permute-start.8 = (bf16[8,512]{1,0:T(8,128)(2,1)S(1)}, bf16[8,512]{1,0:T(8,128)(2,1)S(1)}, u32[]{:S(2)}, u32[]{:S(2)}) collective-permute-start(bf16[8,512]{1,0:T(8,128)(2,1)S(1)} %get-tuple-element.37), channel_id=1, source_target_pairs={{12,0},{0,4},{4,8},{8,12},{13,1},{1,5},{5,9},{9,13},{14,2},{2,6},{... | collective-permute-start | bytes 24584 | tf_op jit(solution)/shard_map/ppermute | solution.py:482
  32.4 4.9 %collective-permute-start.6 = (bf16[8,512]{1,0:T(8,128)(2,1)}, bf16[8,512]{1,0:T(8,128)(2,1)S(1)}, u32[]{:S(2)}, u32[]{:S(2)}) collective-permute-start(bf16[8,512]{1,0:T(8,128)(2,1)} %copy-done.8), channel_id=1, source_target_pairs={{4,0},{8,4},{12,8},{0,12},{5,1},{9,5},{13,9},{1,13},{6,2},{10,6},{... | collective-permute-start | bytes 24584 | tf_op jit(solution)/shard_map/ppermute | solution.py:482
  37.3 2.2 %copy-start.1 = (bf16[512,4096]{1,0:T(8,128)(2,1)S(1)}, bf16[512,4096]{1,0:T(8,128)(2,1)}, u32[]{:S(2)}) copy-start(bf16[512,4096]{1,0:T(8,128)(2,1)} %copy-done) | copy-start | bytes 12582916
  43.6 0.8 %copy-start.3 = (f32[64,2048]{1,0:T(8,128)}, f32[64,2048]{1,0:T(8,128)S(1)}, u32[]{:S(2)}) copy-start(f32[64,2048]{1,0:T(8,128)S(1)} %get-tuple-element.42.refs_0_) | copy-start | bytes 1572868
  44.4 9.0 %copy-start.7 = (bf16[96,2048]{1,0:T(8,128)(2,1)S(1)}, bf16[96,2048]{1,0:T(8,128)(2,1)}, u32[]{:S(2)}) copy-start(bf16[96,2048]{1,0:T(8,128)(2,1)} %copy-done.6) | copy-start | bytes 1179652
  47.7 5.7 %collective-permute-start.9 = (bf16[256,2048]{1,0:T(8,128)(2,1)}, bf16[256,2048]{1,0:T(8,128)(2,1)}, u32[]{:S(2)}, u32[]{:S(2)}) collective-permute-start(bf16[256,2048]{1,0:T(8,128)(2,1)} %get-tuple-element.40), channel_id=1, source_target_pairs={{0,1},{1,0},{2,3},{3,2},{4,5},{5,4},{6,7},{7,6},{8,9},{9,8},{10,11... | collective-permute-start | bytes 3145736 | tf_op jit(solution)/shard_map/ppermute | solution.py:501
  47.8 2.8 %collective-permute-start.11 = (bf16[64,2048]{1,0:T(8,128)(2,1)S(1)}, bf16[64,2048]{1,0:T(8,128)(2,1)}, u32[]{:S(2)}, u32[]{:S(2)}) collective-permute-start(bf16[64,2048]{1,0:T(8,128)(2,1)S(1)} %get-tuple-element.43), channel_id=1, source_target_pairs={{0,1},{1,0},{2,3},{3,2},{4,5},{5,4},{6,7},{7,6},{8,9},{9,8},{10,11... | collective-permute-start | bytes 786440 | tf_op jit(solution)/shard_map/ppermute | solution.py:398
  48.3 0.8 %copy-start.4 = (bf16[96,2048]{1,0:T(8,128)(2,1)}, bf16[96,2048]{1,0:T(8,128)(2,1)S(1)}, u32[]{:S(2)}) copy-start(bf16[96,2048]{1,0:T(8,128)(2,1)S(1)} %collective-permute-done.10.refs_1_) | copy-start | bytes 1179652
  51.8 8.6 %collective-permute-start.12 = (bf16[64,2048]{1,0:T(8,128)(2,1)S(1)}, bf16[64,2048]{1,0:T(8,128)(2,1)S(1)}, u32[]{:S(2)}, u32[]{:S(2)}) collective-permute-start(bf16[64,2048]{1,0:T(8,128)(2,1)S(1)} %add_convert_fusion.2), channel_id=1, source_target_pairs={{0,2},{1,3},{2,0},{3,1},{4,6},{5,7},{6,4},{7,5},{8,10},{9,11},{10,... | collective-permute-start | bytes 786440 | tf_op jit(solution)/shard_map/ppermute | solution.py:404
  53.4 1.0 %copy-start.5 = (bf16[96,2048]{1,0:T(8,128)(2,1)S(1)}, bf16[96,2048]{1,0:T(8,128)(2,1)}, u32[]{:S(2)}) copy-start(bf16[96,2048]{1,0:T(8,128)(2,1)} %copy-done.4) | copy-start | bytes 1179652

commit v3 on v2

v3 whole, which is shorter than its diff:
```python
import functools

import jax
import jax.numpy as jnp
from jax import lax
from jax.experimental import pallas as pl
from jax.experimental.pallas import tpu as pltpu
from jax.sharding import PartitionSpec as P

LOG2E = 1.4426950408889634
MASKED = -1e30
GROUP = 6
NEVER = 2**30

VMEM = pl.BlockSpec(memory_space=pltpu.VMEM)
SMEM = pl.BlockSpec(memory_space=pltpu.SMEM)
ANY = pl.BlockSpec(memory_space=pl.ANY)


def attend_group(queries, tokens, contexts, live_lengths, step_count):
    count = len(queries)
    head_dim = tokens[0].shape[1] // 2
    head_count = queries[0].shape[1] // head_dim
    rows = head_count * step_count
    gain = LOG2E / head_dim**0.5
    stacked = jnp.concatenate(
        [
            query[:, h * head_dim : (h + 1) * head_dim]
            for query in queries
            for h in range(head_count)
        ],
        axis=0,
    ).astype(jnp.bfloat16)
    tokens = jnp.concatenate(tokens, axis=0).astype(jnp.bfloat16)
    score_new = contract_last(stacked, tokens[:, :head_dim])
    row_ids = lax.broadcasted_iota(jnp.int32, score_new.shape, 0)
    column_ids = lax.broadcasted_iota(jnp.int32, score_new.shape, 1)
    allowed = (row_ids // rows == column_ids // step_count) & (
        column_ids % step_count <= row_ids % step_count
    )
    score_new = jnp.where(allowed, score_new, MASKED)
    new_max = jnp.max(score_new, axis=1, keepdims=True)
    maxima, scores = [], []
    for g in range(count):
        keys = jnp.concatenate([page[:, :head_dim] for page in contexts[g]], axis=0)
        score = contract_last(stacked[g * rows : (g + 1) * rows], keys)
        position = lax.broadcasted_iota(jnp.int32, score.shape, 1)
        score = jnp.where(position < live_lengths[g], score, MASKED)
        scores.append(score)
        maxima.append(
            jnp.maximum(
                jnp.max(score, axis=1, keepdims=True), new_max[g * rows : (g + 1) * rows]
            )
        )
    exp_new = jnp.exp2((score_new - jnp.concatenate(maxima, axis=0)) * gain)
    new_total = jnp.sum(exp_new, axis=1, keepdims=True)
    results, inverses = [], []
    for g in range(count):
        exp_ctx = jnp.exp2((scores[g] - maxima[g]) * gain)
        total = jnp.sum(exp_ctx, axis=1, keepdims=True) + new_total[g * rows : (g + 1) * rows]
        inverse = 1.0 / total
        inverses.append(inverse)
        values = jnp.concatenate([page[:, head_dim:] for page in contexts[g]], axis=0)
        results.append(
            jnp.dot(
                (exp_ctx * inverse).astype(jnp.bfloat16),
                values,
                preferred_element_type=jnp.float32,
            )
        )
    weight_new = (exp_new * jnp.concatenate(inverses, axis=0)).astype(jnp.bfloat16)
    result = jnp.concatenate(results, axis=0) + jnp.dot(
        weight_new, tokens[:, head_dim:], preferred_element_type=jnp.float32
    )
    return [
        jnp.concatenate(
            [
                result[g * rows + h * step_count : g * rows + (h + 1) * step_count]
                for h in range(head_count)
            ],
            axis=1,
        )
        for g in range(count)
    ]


def contract_last(a, b):
    return lax.dot_general(a, b, (((1,), (1,)), ((), ())), preferred_element_type=jnp.float32)


def route_of(migration, own_index, peer, arriving):
    ours, theirs, slot_row = (2, 0, 3) if arriving else (0, 2, 1)
    slot = jnp.int32(0)
    for row in range(migration.shape[1]):
        match = (migration[ours, row] == own_index) & (migration[theirs, row] == peer)
        slot = jnp.where(match, migration[slot_row, row], slot)
    return slot


def arrivals_of(migration, inst_count):
    me = lax.axis_index("inst")
    incoming = migration.shape[1] // inst_count
    slots = [jnp.int32(NEVER)] * incoming
    sources = [jnp.int32(0)] * incoming
    for row in range(migration.shape[1]):
        slot = jnp.where(migration[2, row] == me, migration[3, row], NEVER)
        source = migration[0, row]
        for i in range(incoming):
            before = slot < slots[i]
            slots[i], slot = jnp.where(before, slot, slots[i]), jnp.where(before, slots[i], slot)
            sources[i], source = (
                jnp.where(before, source, sources[i]),
                jnp.where(before, sources[i], source),
            )
    return slots, sources


def slot_at(position, arrivals, slot_count):
    kept = slot_count - len(arrivals)
    if position >= kept:
        return jnp.minimum(arrivals[position - kept], slot_count - 1)
    slot = jnp.int32(position)
    for arrival in arrivals:
        slot = slot + (slot >= arrival).astype(jnp.int32)
    return slot


def pack_rows(inst_count, migration, queries, new_tokens, packs):
    me = lax.axis_index("inst")
    width = queries.shape[2]
    for peer in range(inst_count):
        slot = route_of(migration, me, peer, True)
        packs[peer, :, :width] = queries[slot]
        packs[peer, :, width:] = new_tokens[slot]


def page_copies(pool, buffer, sems, page_table, item, slot):
    page_count = page_table.shape[0]
    for j in range(page_count):
        pltpu.make_async_copy(
            pool.at[page_table[j, slot]], buffer.at[item, j], sems.at[item]
        ).start()


def wait_copies(pool, buffer, sems, item):
    pltpu.make_async_copy(
        pool.at[pl.ds(0, buffer.shape[1])], buffer.at[item], sems.at[item]
    ).wait()


def away_kernel(inst_count, lengths, page_table, migration, after, received, pool, answers, buffer, sems):
    count = inst_count - 1
    page_count, slot_count = page_table.shape
    page_len = pool.shape[1]
    me = lax.axis_index("inst")
    _, step_count, width = answers.shape
    peers = [lax.rem(me + k, inst_count) for k in range(1, inst_count)]
    live = []
    for k, peer in enumerate(peers):
        slot = route_of(migration, me, peer, False)
        page_copies(pool, buffer, sems, page_table, k, slot)
        live.append(lengths[me * slot_count + slot] * page_len)
    items = [received[peer].astype(jnp.float32) for peer in peers]
    for k in range(count):
        wait_copies(pool, buffer, sems, k)
    result = attend_group(
        [item[:, :width] for item in items],
        [item[:, width:] for item in items],
        [[buffer.at[k, j] for j in range(page_count)] for k in range(count)],
        live,
        step_count,
    )
    answers[me] = jnp.zeros((step_count, width), answers.dtype)
    for peer, rows in zip(peers, result):
        answers[peer] = rows.astype(answers.dtype)


def project(rows, weight, first, columns, target, row_offset=0, offset=0):
    tile = min(512, columns)
    rows = rows[...]
    for j in range(0, columns, tile):
        start = pl.multiple_of(first + j, tile)
        target[row_offset : row_offset + rows.shape[0], offset + j : offset + j + tile] = jnp.dot(
            rows, weight[:, pl.ds(start, tile)], preferred_element_type=jnp.float32
        ).astype(target.dtype)


def project_far(attended, far_weight, keep, send):
    core = lax.rem(lax.axis_index("tp"), 2)
    chips = lax.axis_size("tp") // 2
    columns = far_weight.shape[1] // (2 * chips - 2)
    for target, side in ((send, 1 - core), (keep, core)):
        for d in range(chips - 1):
            first = (2 * d + side) * columns
            project(attended, far_weight, first, columns, target, 0, d * columns)


def attend_slots(
    inst_count, positions, migration, lengths, page_table, queries, new_tokens, pool, buffer, sems,
    between=lambda: None,
):
    page_count, slot_count = page_table.shape
    page_len = pool.shape[1]
    me = lax.axis_index("inst")
    arrivals, _ = arrivals_of(migration, inst_count)
    slots = [slot_at(position, arrivals, slot_count) for position in positions]
    for i, slot in enumerate(slots):
        page_copies(pool, buffer, sems, page_table, i, slot)
    between()
    rows = []
    for base in range(0, len(slots), GROUP):
        items = range(base, min(base + GROUP, len(slots)))
        for i in items:
            wait_copies(pool, buffer, sems, i)
        rows += attend_group(
            [queries[slots[i]].astype(jnp.float32) for i in items],
            [new_tokens[slots[i]].astype(jnp.float32) for i in items],
            [[buffer.at[i, j] for j in range(page_count)] for i in items],
            [lengths[me * slot_count + slots[i]] * page_len for i in items],
            queries.shape[1],
        )
    return rows


def store_rows(rows, target, at=0):
    step_count = rows[0].shape[0]
    for pair in range(0, len(rows), 2):
        start = at + pair * step_count
        target[start : start + 2 * step_count, :] = jnp.concatenate(
            rows[pair : pair + 2], axis=0
        ).astype(jnp.bfloat16)


def first_kernel(
    inst_count, migration, lengths, page_table, queries, new_tokens, pool, weight,
    attended, keep, send, far_weight, packs, buffer, page_sems, weight_sems,
):
    own_tp = lax.axis_index("tp")
    chips = lax.axis_size("tp") // 2
    pair_columns = weight.shape[1] // chips

    def weight_copy(d):
        chip = lax.rem(own_tp // 2 + d, chips)
        start = pl.multiple_of(chip * pair_columns, pair_columns)
        return pltpu.make_async_copy(
            weight.at[:, pl.ds(start, pair_columns)],
            far_weight.at[:, pl.ds((d - 1) * pair_columns, pair_columns)],
            weight_sems.at[d - 1],
        )

    def between():
        for d in range(1, chips):
            weight_copy(d).start()
        pack_rows(inst_count, migration, queries, new_tokens, packs)

    count = attended.shape[0] // queries.shape[1]
    store_rows(
        attend_slots(
            inst_count, range(count), migration, lengths, page_table, queries, new_tokens, pool,
            buffer, page_sems, between,
        ),
        attended,
    )
    for d in range(1, chips):
        weight_copy(d).wait()
    project_far(attended, far_weight, keep, send)


def second_kernel(
    inst_count, first, migration, lengths, page_table, queries, new_tokens, pool, far_weight,
    after, attended, extra, keep, send, buffer, sems,
):
    count = attended.shape[0] // queries.shape[1]
    rows = attend_slots(
        inst_count, range(first, first + count + extra.shape[0]), migration, lengths, page_table,
        queries, new_tokens, pool, buffer, sems,
    )
    store_rows(rows[:count], attended)
    for i, row in enumerate(rows[count:]):
        extra[i] = row.astype(extra.dtype)
    project_far(attended, far_weight, keep, send)


def own_kernel(weight, first, second, keep, send, near_weight, rows, sems):
    core = lax.rem(lax.axis_index("tp"), 2)
    chip = lax.axis_index("tp") // 2
    columns = keep.shape[1]
    copies = []
    for n, side in enumerate((1 - core, core)):
        start = pl.multiple_of((chip * 2 + side) * columns, columns)
        copies.append(
            pltpu.make_async_copy(
                weight.at[:, pl.ds(start, columns)], near_weight.at[n], sems.at[n]
            )
        )
        copies[n].start()
    rows[: first.shape[0], :] = first[...]
    rows[first.shape[0] :, :] = second[...]
    for n, target in enumerate((send, keep)):
        copies[n].wait()
        project(rows, near_weight.at[n], 0, columns, target)


def last_rows_kernel(
    inst_count, migration, near_weight, far_weight, extra, answers, keep, send, rows
):
    core = lax.rem(lax.axis_index("tp"), 2)
    chips = lax.axis_size("tp") // 2
    columns = keep.shape[1]
    _, sources = arrivals_of(migration, inst_count)
    last = [extra[i].astype(jnp.float32) for i in range(extra.shape[0])]
    last += [answers[source].astype(jnp.float32) for source in sources]
    size = rows.shape[0]
    store_rows(last, rows)
    for n, (target, side) in enumerate(((send, 1 - core), (keep, core))):
        for d in range(chips - 1):
            project(rows, far_weight, (2 * d + side) * columns, columns, target, d * size)
        project(rows, near_weight.at[n], 0, columns, target, (chips - 1) * size)


def sum_kernel(inst_count, chunks, migration, keep, mate, *refs):
    (out, staged, sem), parts = refs[-3:], refs[:-3]
    slot_count, step_count, _ = out.shape
    pair = 2 * step_count
    arrivals, _ = arrivals_of(migration, inst_count)
    share = len(parts) // len(chunks)
    at = 0
    for n, chunk in enumerate(chunks):
        for base in range(0, chunk, pair):
            total = keep[at : at + pair, :] + mate[at : at + pair, :].astype(jnp.float32)
            for part in parts[n * share : (n + 1) * share]:
                total = total + part[base : base + pair, :].astype(jnp.float32)
            total = total.astype(jnp.bfloat16)
            for half in range(2):
                staged[at // step_count + half] = total[half * step_count : (half + 1) * step_count]
            at += pair
    scatter_rows(staged, out, arrivals, 0, sem)


def scatter_rows(staged, out, arrivals, first, sem):
    slot_count = out.shape[0]
    for i in range(staged.shape[0]):
        slot = slot_at(first + i, arrivals, slot_count)
        pltpu.make_async_copy(staged.at[i], out.at[slot], sem.at[0]).start()
    pltpu.make_async_copy(staged, out.at[pl.ds(0, staged.shape[0])], sem.at[0]).wait()


def last_kernel(inst_count, first, migration, keep, mate, *refs):
    parts, (out, staged, sem) = refs[:-4], refs[-3:]
    step_count = out.shape[1]
    pair = 2 * step_count
    size = parts[0].shape[0]
    arrivals, _ = arrivals_of(migration, inst_count)
    for at in range(0, size, pair):
        own = keep.shape[0] - size + at
        total = keep[own : own + pair, :] + mate[own : own + pair, :].astype(jnp.float32)
        for part in parts:
            total = total + part[at : at + pair, :].astype(jnp.float32)
        total = total.astype(jnp.bfloat16)
        for half in range(2):
            staged[at // step_count + half] = total[half * step_count : (half + 1) * step_count]
    scatter_rows(staged, out, arrivals, first, sem)


def in_hbm(value):
    return pltpu.with_memory_space_constraint(value, pltpu.HBM)


def in_vmem(value):
    return pltpu.with_memory_space_constraint(value, pltpu.VMEM)


def on_device(queries, new_kv, kv_pool, out_weight, lengths, page_table, migration):
    inst_count = lax.axis_size("inst")
    tp_count = lax.axis_size("tp")
    chips = tp_count // 2
    slot_count, page_count = page_table.shape
    row_count, width = queries.shape
    step_count = row_count // slot_count
    queries = in_hbm(queries.reshape(slot_count, step_count, width))
    new_tokens = in_hbm(new_kv[0].reshape(slot_count, step_count, new_kv.shape[2]))
    pool = in_hbm(kv_pool[0])
    page_shape = pool.shape[1:]
    columns = out_weight.shape[1] // tp_count
    incoming = migration.shape[0] // inst_count
    weight = in_hbm(out_weight)
    lengths = in_hbm(lengths)
    page_table = in_hbm(page_table.T)
    migration = in_hbm(migration.T)
    limit = pltpu.CompilerParams(vmem_limit_bytes=32 * 2**20)
    light = pl.CostEstimate(flops=1, bytes_accessed=1, transcendentals=0)
    bf16, f32 = jnp.bfloat16, jnp.float32
    shape = jax.ShapeDtypeStruct
    swap = [(t, t ^ 1) for t in range(tp_count)]
    far = (chips - 1) * columns

    def hold(value, until):
        return pl.pallas_call(
            lambda *refs: None,
            out_shape=pltpu.VMEM(value.shape, value.dtype),
            in_specs=[ANY] * (1 + len(until)),
            out_specs=ANY,
            input_output_aliases={0: 0},
            compiler_params=pltpu.CompilerParams(vmem_limit_bytes=2**20),
            cost_estimate=light,
            name="hold",
        )(in_vmem(value), *until)

    def send_far(summed):
        return [
            lax.ppermute(
                part, "tp", [(t, (t + 2 * d) % tp_count) for t in range(tp_count)]
            )
            for d, part in enumerate(summed, 1)
        ]

    def split_far(summed):
        return [summed[:, d * columns : (d + 1) * columns] for d in range(chips - 1)]

    def chunk_shapes(count):
        rows = count * step_count
        return [pltpu.VMEM((rows, far), f32), pltpu.VMEM((rows, far), bf16)]

    def rows_shape(count):
        return pltpu.VMEM((count * step_count, width), bf16)

    def page_scratch(count):
        return [
            pltpu.VMEM((count, page_count, *page_shape), bf16),
            pltpu.SemaphoreType.DMA((count,)),
        ]

    last_count = incoming + incoming % 2
    extra_count = last_count - incoming
    first_count = slot_count // 4 * 2
    second_count = slot_count - first_count - last_count
    last_rows = last_count * step_count

    first, keep, send, far_weight, packs = pl.pallas_call(
        functools.partial(first_kernel, inst_count),
        out_shape=[
            rows_shape(first_count),
            *chunk_shapes(first_count),
            pltpu.VMEM((width, 2 * far), bf16),
            shape((inst_count, step_count, width + new_tokens.shape[2]), bf16),
        ],
        in_specs=[SMEM, SMEM, SMEM, VMEM, VMEM, ANY, ANY],
        out_specs=[VMEM] * 5,
        scratch_shapes=page_scratch(first_count) + [pltpu.SemaphoreType.DMA((chips - 1,))],
        compiler_params=limit,
        cost_estimate=light,
        name="attend_first",
    )(migration, lengths, page_table, queries, new_tokens, pool, weight)
    far_weight = in_vmem(far_weight)
    mate = lax.ppermute(send, "tp", swap)
    summed = (keep + mate.astype(f32)).astype(bf16)
    arrived_first = send_far(split_far(summed))
    received = lax.all_to_all(packs, "inst", split_axis=0, concat_axis=0, tiled=True)

    second, extra, keep, send = pl.pallas_call(
        functools.partial(second_kernel, inst_count, first_count),
        out_shape=[
            rows_shape(second_count),
            pltpu.VMEM((extra_count, step_count, width), bf16),
            *chunk_shapes(second_count),
        ],
        in_specs=[SMEM, SMEM, SMEM, VMEM, VMEM, ANY, VMEM, ANY],
        out_specs=[VMEM] * 4,
        scratch_shapes=page_scratch(second_count + extra_count),
        compiler_params=limit,
        cost_estimate=light,
        name="attend_second",
    )(migration, lengths, page_table, queries, new_tokens, pool, far_weight, summed)
    mate = lax.ppermute(send, "tp", swap)
    answers = pl.pallas_call(
        functools.partial(away_kernel, inst_count),
        out_shape=shape((inst_count, step_count, width), bf16),
        in_specs=[SMEM, SMEM, SMEM, ANY, VMEM, ANY],
        out_specs=VMEM,
        scratch_shapes=page_scratch(inst_count - 1),
        compiler_params=limit,
        cost_estimate=light,
        name="attend_away",
    )(lengths, page_table, migration, second, received, pool)
    early_rows = (first_count + second_count) * step_count
    early_keep, early_send, near_weight = pl.pallas_call(
        own_kernel,
        out_shape=[
            pltpu.VMEM((early_rows, columns), f32),
            pltpu.VMEM((early_rows, columns), bf16),
            pltpu.VMEM((2, width, columns), bf16),
        ],
        in_specs=[ANY, VMEM, VMEM],
        out_specs=[VMEM] * 3,
        scratch_shapes=[
            pltpu.VMEM((early_rows, width), bf16),
            pltpu.SemaphoreType.DMA((2,)),
        ],
        compiler_params=limit,
        cost_estimate=light,
        name="own_columns",
    )(weight, in_vmem(first), in_vmem(second))
    early_mate = lax.ppermute(early_send, "tp", swap)
    keep = hold(keep, [*arrived_first, answers, early_keep])
    summed = (keep + mate.astype(f32)).astype(bf16)
    arrived_second = send_far(split_far(summed))
    answers = lax.all_to_all(answers, "inst", split_axis=0, concat_axis=0, tiled=True)

    keep, send = pl.pallas_call(
        functools.partial(last_rows_kernel, inst_count),
        out_shape=[
            pltpu.VMEM((last_rows * chips, columns), f32),
            pltpu.VMEM((last_rows * chips, columns), bf16),
        ],
        in_specs=[SMEM] + [VMEM] * 4,
        out_specs=[VMEM] * 2,
        scratch_shapes=[pltpu.VMEM((last_rows, width), bf16)],
        compiler_params=limit,
        cost_estimate=light,
        name="last_rows",
    )(migration, in_vmem(near_weight), far_weight, in_vmem(extra), answers)
    mate = lax.ppermute(send, "tp", swap)
    keep = hold(keep, arrived_second)
    summed = (keep[:-last_rows] + mate[:-last_rows].astype(f32)).astype(bf16)
    arrived_last = send_far([summed[d * last_rows : (d + 1) * last_rows] for d in range(chips - 1)])

    early = slot_count - last_count
    out_shape = (slot_count, step_count, columns)
    out = pl.pallas_call(
        functools.partial(
            sum_kernel, inst_count, [first_count * step_count, second_count * step_count]
        ),
        out_shape=pltpu.HBM(out_shape, bf16),
        in_specs=[SMEM] + [VMEM] * (2 + 2 * (chips - 1)),
        out_specs=ANY,
        scratch_shapes=[
            pltpu.VMEM((early, step_count, columns), bf16),
            pltpu.SemaphoreType.DMA((1,)),
        ],
        compiler_params=limit,
        cost_estimate=light,
        name="sum_early",
    )(migration, in_vmem(early_keep), early_mate, *arrived_first, *arrived_second)
    out = pl.pallas_call(
        functools.partial(last_kernel, inst_count, early),
        out_shape=pltpu.HBM(out_shape, bf16),
        in_specs=[SMEM] + [VMEM] * (chips + 1) + [ANY],
        out_specs=ANY,
        scratch_shapes=[
            pltpu.VMEM((last_count, step_count, columns), bf16),
            pltpu.SemaphoreType.DMA((1,)),
        ],
        input_output_aliases={2 + chips: 0},
        compiler_params=limit,
        cost_estimate=light,
        name="sum_last",
    )(migration, in_vmem(keep), mate, *arrived_last, out)
    return out.reshape(row_count, columns)


def solution(mesh):
    placed = (
        P(("group", "inst"), "tp"),
        P("tp", ("group", "inst"), None),
        P("tp", ("group", "inst"), None, None),
        P("tp", None),
        P("group"),
        P(("group", "inst"), None),
        P("group", None),
    )
    return jax.shard_map(
        on_device, mesh=mesh, in_specs=placed, out_specs=P(("group", "inst"), "tp"), check_vma=False
    )
```

time: 62.4 us -> 55.3 us (0.89)
  blocking collectives: 0 us -> 10.5 us
  waiting for transfers between devices: 13 us -> 5.18 us
  starting transfers between devices: 14.8 us -> 10.5 us
  local copies, waits for them, and re-layouts: 6.12 us -> 2.92 us
  Pallas kernels: 25.4 us -> 23.4 us
    ppermute x12 -> x4, waiting for transfers between devices: 13 us -> 2.12 us  [the longest x3 2.12 us: send_far(): lax.ppermute(part, 'tp', [(t, (t + 2 * d) % tp_count) for t in range(tp_c...]
    all_to_all x0 -> x1, blocking collectives: none -> 10.5 us  [on_device(): lax.all_to_all(answers, 'inst', split_axis=0, concat_axis=0, tiled=True)]
    ppermute x12 -> x4, starting transfers between devices: 14.7 us -> 5.05 us  [the longest x3 5.04 us: send_far(): lax.ppermute(part, 'tp', [(t, (t + 2 * d) % tp_count) for t in range(tp_c...]
    all_to_all x0 -> x1, starting transfers between devices: none -> 4.87 us  [on_device(): lax.all_to_all(packs, 'inst', split_axis=0, concat_axis=0, tiled=True)]
    unnamed x18 -> x12, local copies, waits for them, and re-layouts: 6.12 us -> 2.92 us
    ppermute x1 -> x3, waiting for transfers between devices: 0.01 us -> 3.06 us  [on_device(): mate = lax.ppermute(send, 'tp', swap)]
    pallas_call x9 -> x8, Pallas kernels: 23.9 us -> 22 us  [the longest x1 5.93 us: on_device(): pl.pallas_call(functools.partial(second_kernel, inst_count, first_count),...]
  transfers between devices with their start and end apart: 13 -> 8, of which waited for: 7 -> 3; matrix products, arithmetic and copies ran while one was open for 2% -> 0% of each run, Pallas kernels for 28% -> 29%
where the time goes in v3:
time: 55.3 us; the launch traced here: 54.9 us
  Pallas kernels  23.4 us (42%)
  starting transfers between devices  10.5 us (19%)
  blocking collectives  10.5 us (19%)
  waiting for transfers between devices  5.18 us (9%)
  local copies, waits for them, and re-layouts  2.92 us (5%)
  other arithmetic  2.2 us (4%)
    all_to_all x1, blocking collectives, on_device(): lax.all_to_all(answers, 'inst', split_axis=0, concat_axis=0, tiled=True)  10.5 us
    pallas_call x1, Pallas kernels, on_device(): pl.pallas_call(functools.partial(second_kernel, inst_count, first_count),...  5.93 us
    pallas_call x1, Pallas kernels, on_device(): pl.pallas_call(functools.partial(first_kernel, inst_count), out_shape=[ro...  5.88 us
    ppermute x3, starting transfers between devices, send_far(): lax.ppermute(part, 'tp', [(t, (t + 2 * d) % tp_count) for t in range(tp_c...  5.04 us
    all_to_all x1, starting transfers between devices, on_device(): lax.all_to_all(packs, 'inst', split_axis=0, concat_axis=0, tiled=True)  4.87 us
    pallas_call x1, Pallas kernels, on_device(): pl.pallas_call(functools.partial(away_kernel, inst_count), out_shape=shap...  3.12 us
    ppermute x3, waiting for transfers between devices, on_device(): mate = lax.ppermute(send, 'tp', swap)  3.06 us
    unnamed x12, local copies, waits for them, and re-layouts  2.92 us
  transfers between devices with their start and end apart: 8, of which 3 were waited for; matrix products, arithmetic and copies ran while one was open for 0% of the time, Pallas kernels for 29%

profile of v3, /device:TPU:0, one launch (start us, length us, event | category | flops | bytes accessed | tf_op | source)
XLA Modules:
  0.0 54.9 jit_solution(13278067184413457772)
XLA Ops:
  0.0 5.9 %attend_first.1 = (bf16[128,512]{1,0:T(8,128)(2,1)S(1)}, f32[128,2048]{1,0:T(8,128)S(1)}, bf16[128,2048]{1,0:T(8,128)(2,1)S(1)}, bf16[512,4096]{1,0:T(8,128)(2,1)S(1)}, bf16[4,8,768]{2,1,0:T(8,128)(2,1)}) custom-call(s32[4,12]{1,0:T(4,128)} %bitcast.13, s32[128]{0:T(128)} %lengths.5, s32[4,32]{1,0:T(4,128)} %bitcast.19, bf16[32,8,512]{2,1,0:T(8,128)(2,1)} %bitcast.9, ...), custom_call_target="tpu_custom_call" | custom-call | flops 1 | bytes 1 | tf_op jit(solution)/shard_map/attend_first/pallas_call | solution.py:439
  5.9 0.0 copy-start
  5.9 0.5 collective-permute-start
  6.4 1.5 %collective-permute-done = bf16[128,2048]{1,0:T(8,128)(2,1)S(1)} collective-permute-done((bf16[128,2048]{1,0:T(8,128)(2,1)S(1)}, bf16[128,2048]{1,0:T(8,128)(2,1)S(1)}, u32[]{:S(2)}, u32[]{:S(2)}) %collective-permute-start) | collective-permute-done | bytes 524320 | tf_op jit(solution)/shard_map/ppermute | solution.py:455
  8.0 0.9 %add_convert_fusion.after = bf16[128,2048]{1,0:T(8,128)(2,1)} fusion(f32[128,2048]{1,0:T(8,128)S(1)} %get-tuple-element.21, bf16[128,2048]{1,0:T(8,128)(2,1)S(1)} %collective-permute-done), kind=kLoop, calls=%fused_computation | loop fusion | flops 786432 | bytes 2097152 | tf_op jit(solution)/shard_map/convert_element_type | solution.py:456
  8.9 2.9 %collective-permute-start.1 = (bf16[128,2048]{1,0:T(8,128)(2,1)}, bf16[128,2048]{1,0:T(8,128)(2,1)S(1)}, u32[]{:S(2)}, u32[]{:S(2)}) collective-permute-start(bf16[128,2048]{1,0:T(8,128)(2,1)} %add_convert_fusion.after), channel_id=1, source_target_pairs={{0,2},{1,3},{2,0},{3,1},{4,6},{5,7},{6,4},{7,5},{8,10},{9,11},{10,... | collective-permute-start | bytes 1572872 | tf_op jit(solution)/shard_map/ppermute | solution.py:411
  11.8 5.9 %attend_second.1 = (bf16[96,512]{1,0:T(8,128)(2,1)S(1)}, bf16[1,8,512]{2,1,0:T(8,128)(2,1)S(1)}, f32[96,2048]{1,0:T(8,128)S(1)}, bf16[96,2048]{1,0:T(8,128)(2,1)}) custom-call(s32[4,12]{1,0:T(4,128)} %bitcast.14, s32[128]{0:T(128)} %lengths.5, s32[4,32]{1,0:T(4,128)} %bitcast.20, bf16[32,8,512]{2,1,0:T(8,128)(2,1)} %bitcast.10, ...), custom_call_target="tpu_custom_call" | custom-call | flops 1 | bytes 1 | tf_op jit(solution)/shard_map/attend_second/pallas_call | solution.py:460
  17.7 0.0 copy-done
  17.7 0.1 collective-permute-start.2
  17.8 4.9 %all-to-all-start = ((bf16[4,8,768]{2,1,0:T(8,128)(2,1)}), bf16[4,8,768]{2,1,0:T(8,128)(2,1)S(1)}, u32[]{:S(2)}, u32[]{:S(2)}) async-start(bf16[4,8,768]{2,1,0:T(8,128)(2,1)} %get-tuple-element.26), calls=%async_computation | async-start | bytes 98304 | tf_op jit(solution)/shard_map/all_to_all | solution.py:458
  22.7 2.9 %own_columns.1 = (f32[224,2048]{1,0:T(8,128)S(1)}, bf16[224,2048]{1,0:T(8,128)(2,1)S(1)}, bf16[2,512,2048]{2,1,0:T(8,128)(2,1)S(1)}) custom-call(bf16[512,8192]{1,0:T(8,128)(2,1)} %weight.3, bf16[128,512]{1,0:T(8,128)(2,1)S(1)} %get-tuple-element.19.first, bf16[96,512]{1,0:T(8,128)(2,1)S(1)} %get-tuple-element.23.second.after), custom_call_target="tpu_custom_call" | custom-call | flops 1 | bytes 1 | tf_op jit(solution)/shard_map/own_columns/pallas_call | solution.py:486
  25.6 0.0 copy-start.2
  25.6 2.0 %copy-done.2 = bf16[2,512,2048]{2,1,0:T(8,128)(2,1)} copy-done((bf16[2,512,2048]{2,1,0:T(8,128)(2,1)}, bf16[2,512,2048]{2,1,0:T(8,128)(2,1)S(1)}, u32[]{:S(2)}) %copy-start.2) | copy-done | bytes 4194328
  27.6 0.0 copy-start.4
  27.6 0.9 %copy-done.4 = bf16[224,2048]{1,0:T(8,128)(2,1)} copy-done((bf16[224,2048]{1,0:T(8,128)(2,1)}, bf16[224,2048]{1,0:T(8,128)(2,1)S(1)}, u32[]{:S(2)}) %copy-start.4) | copy-done | bytes 917528
  28.5 0.0 all-to-all-done.received
  28.5 0.0 copy-start.3
  28.5 3.1 %attend_away.1.refs_2_ = bf16[4,8,512]{2,1,0:T(8,128)(2,1)S(1)} custom-call(s32[128]{0:T(128)} %lengths.5, s32[4,32]{1,0:T(4,128)} %bitcast.21, s32[4,12]{1,0:T(4,128)} %bitcast.15, bf16[96,512]{1,0:T(8,128)(2,1)S(1)} %get-tuple-element.23.second.after, bf16[4,8,768]{2,1,0:T(8,128)(2,1)S(1)} %all-to-all-done.received, bf16[128,128,256]{2,1,0:T(8,128)(2,1)} %bitcast.8), custom_call_target="tpu_custom_call" | custom-call | flops 1 | bytes 1 | tf_op jit(solution)/shard_map/attend_away/pallas_call | solution.py:475
  31.7 0.0 copy-start.5
  31.7 0.0 copy-start.1
  31.7 0.0 collective-permute-done.1.refs_1_.refs_0_
  31.7 0.0 collective-permute-done.2
  31.7 1.2 %add_convert_fusion.1 = bf16[96,2048]{1,0:T(8,128)(2,1)S(1)} fusion(f32[96,2048]{1,0:T(8,128)S(1)} %hold.2, bf16[96,2048]{1,0:T(8,128)(2,1)} %collective-permute-done.2), kind=kLoop, calls=%fused_computation.1 | loop fusion | flops 589824 | bytes 1572864 | tf_op jit(solution)/shard_map/convert_element_type | solution.py:505
  32.9 0.6 %collective-permute-start.3 = (bf16[96,2048]{1,0:T(8,128)(2,1)S(1)}, bf16[96,2048]{1,0:T(8,128)(2,1)S(1)}, u32[]{:S(2)}, u32[]{:S(2)}) collective-permute-start(bf16[96,2048]{1,0:T(8,128)(2,1)S(1)} %add_convert_fusion.1), channel_id=1, source_target_pairs={{0,2},{1,3},{2,0},{3,1},{4,6},{5,7},{6,4},{7,5},{8,10},{9,11},{10,... | collective-permute-start | bytes 1179656 | tf_op jit(solution)/shard_map/ppermute | solution.py:411
  33.5 0.0 copy-done.5
  33.5 0.0 collective-permute-start.6
  33.5 10.5 %all_to_all.10.answers = bf16[4,8,512]{2,1,0:T(8,128)(2,1)S(1)} all-to-all(bf16[4,8,512]{2,1,0:T(8,128)(2,1)S(1)} %attend_away.1.refs_2_), channel_id=1, replica_groups=mesh['group'=2,'inst'=4,'tp'=4] {'inst'}, dimensions={0} | all-to-all | bytes 65536 | tf_op jit(solution)/shard_map/all_to_all | solution.py:507
  44.1 0.0 copy-done.3
  44.1 0.0 copy-done.1
  44.1 2.3 %last_rows.1 = (f32[64,2048]{1,0:T(8,128)S(1)}, bf16[64,2048]{1,0:T(8,128)(2,1)S(1)}) custom-call(s32[4,12]{1,0:T(4,128)} %bitcast.16, bf16[2,512,2048]{2,1,0:T(8,128)(2,1)S(1)} %copy-done.3, bf16[512,4096]{1,0:T(8,128)(2,1)S(1)} %copy-done.1, bf16[1,8,512]{2,1,0:T(8,128)(2,1)S(1)} %get-tuple-element.25.extra, bf16[4,8,512]{2,1,0:T(8,128)(2,1)S(1)} %all_to_all.10.answers), custom_call_target="tpu_custom_call" | custom-call | flops 1 | bytes 1 | tf_op jit(solution)/shard_map/last_rows/pallas_call | solution.py:509
  46.3 0.0 collective-permute-start.4
  46.3 0.0 collective-permute-done.3.refs_1_
  46.4 1.5 %collective-permute-done.4.mate = bf16[64,2048]{1,0:T(8,128)(2,1)S(1)} collective-permute-done((bf16[64,2048]{1,0:T(8,128)(2,1)S(1)}, bf16[64,2048]{1,0:T(8,128)(2,1)S(1)}, u32[]{:S(2)}, u32[]{:S(2)}) %collective-permute-start.4) | collective-permute-done | bytes 262176 | tf_op jit(solution)/shard_map/ppermute | solution.py:522
  47.9 1.6 %collective-permute-start.5 = (bf16[32,2048]{1,0:T(8,128)(2,1)S(1)}, bf16[32,2048]{1,0:T(8,128)(2,1)S(1)}, u32[]{:S(2)}, u32[]{:S(2)}) collective-permute-start(bf16[32,2048]{1,0:T(8,128)(2,1)S(1)} %fusion), channel_id=1, source_target_pairs={{0,2},{1,3},{2,0},{3,1},{4,6},{5,7},{6,4},{7,5},{8,10},{9,11},{10,... | collective-permute-start | bytes 393224 | tf_op jit(solution)/shard_map/ppermute | solution.py:411
  49.5 0.0 collective-permute-done.6.mate
  49.5 1.9 %sum_early.1.refs_1_ = bf16[32,8,2048]{2,1,0:T(8,128)(2,1)} custom-call(s32[4,12]{1,0:T(4,128)} %bitcast.17, f32[224,2048]{1,0:T(8,128)S(1)} %get-tuple-element.29.refs_3_.keep, bf16[224,2048]{1,0:T(8,128)(2,1)S(1)} %collective-permute-done.6.mate, bf16[128,2048]{1,0:T(8,128)(2,1)S(1)} %collective-permute-done.1.refs_1_.refs_0_, ...), custom_call_target="tpu_custom_call" | custom-call | flops 1 | bytes 1 | tf_op jit(solution)/shard_map/sum_early/pallas_call | solution.py:529
  51.4 2.1 %collective-permute-done.5.refs_0_ = bf16[32,2048]{1,0:T(8,128)(2,1)S(1)} collective-permute-done((bf16[32,2048]{1,0:T(8,128)(2,1)S(1)}, bf16[32,2048]{1,0:T(8,128)(2,1)S(1)}, u32[]{:S(2)}, u32[]{:S(2)}) %collective-permute-start.5) | collective-permute-done | bytes 131104 | tf_op jit(solution)/shard_map/ppermute | solution.py:411
  53.5 1.4 %sum_last.1 = bf16[32,8,2048]{2,1,0:T(8,128)(2,1)} custom-call(s32[4,12]{1,0:T(4,128)} %bitcast.18, f32[64,2048]{1,0:T(8,128)S(1)} %hold.3.keep, bf16[64,2048]{1,0:T(8,128)(2,1)S(1)} %collective-permute-done.4.mate, bf16[32,2048]{1,0:T(8,128)(2,1)S(1)} %collective-permute-done.5.refs_0_, ...), custom_call_target="tpu_custom_call", output_to_operand_aliasing={{}: (4, {})} | custom-call | flops 1 | bytes 1 | tf_op jit(solution)/shard_map/sum_last/pallas_call | solution.py:544
  (3 shorter events, 0.0 us)
Async XLA Ops:
  5.9 11.8 %copy-start = (bf16[512,4096]{1,0:T(8,128)(2,1)}, bf16[512,4096]{1,0:T(8,128)(2,1)S(1)}, u32[]{:S(2)}) copy-start(bf16[512,4096]{1,0:T(8,128)(2,1)S(1)} %get-tuple-element.20.far_weight) | copy-start | bytes 12582916
  5.9 2.1 %collective-permute-start = (bf16[128,2048]{1,0:T(8,128)(2,1)S(1)}, bf16[128,2048]{1,0:T(8,128)(2,1)S(1)}, u32[]{:S(2)}, u32[]{:S(2)}) collective-permute-start(bf16[128,2048]{1,0:T(8,128)(2,1)S(1)} %get-tuple-element.22), channel_id=1, source_target_pairs={{0,1},{1,0},{2,3},{3,2},{4,5},{5,4},{6,7},{7,6},{8,9},{9,8},{10,11... | collective-permute-start | bytes 1572872 | tf_op jit(solution)/shard_map/ppermute | solution.py:455
  8.9 22.8 %collective-permute-start.1 = (bf16[128,2048]{1,0:T(8,128)(2,1)}, bf16[128,2048]{1,0:T(8,128)(2,1)S(1)}, u32[]{:S(2)}, u32[]{:S(2)}) collective-permute-start(bf16[128,2048]{1,0:T(8,128)(2,1)} %add_convert_fusion.after), channel_id=1, source_target_pairs={{0,2},{1,3},{2,0},{3,1},{4,6},{5,7},{6,4},{7,5},{8,10},{9,11},{10,... | collective-permute-start | bytes 1572872 | tf_op jit(solution)/shard_map/ppermute | solution.py:411
  17.7 14.0 %collective-permute-start.2 = (bf16[96,2048]{1,0:T(8,128)(2,1)}, bf16[96,2048]{1,0:T(8,128)(2,1)}, u32[]{:S(2)}, u32[]{:S(2)}) collective-permute-start(bf16[96,2048]{1,0:T(8,128)(2,1)} %get-tuple-element.30), channel_id=1, source_target_pairs={{0,1},{1,0},{2,3},{3,2},{4,5},{5,4},{6,7},{7,6},{8,9},{9,8},{10,11... | collective-permute-start | bytes 1179656 | tf_op jit(solution)/shard_map/ppermute | solution.py:474
  17.8 10.7 %all-to-all-start = ((bf16[4,8,768]{2,1,0:T(8,128)(2,1)}), bf16[4,8,768]{2,1,0:T(8,128)(2,1)S(1)}, u32[]{:S(2)}, u32[]{:S(2)}) async-start(bf16[4,8,768]{2,1,0:T(8,128)(2,1)} %get-tuple-element.26), calls=%async_computation | async-start | bytes 98304 | tf_op jit(solution)/shard_map/all_to_all | solution.py:458
  25.6 2.0 %copy-start.2 = (bf16[2,512,2048]{2,1,0:T(8,128)(2,1)}, bf16[2,512,2048]{2,1,0:T(8,128)(2,1)S(1)}, u32[]{:S(2)}) copy-start(bf16[2,512,2048]{2,1,0:T(8,128)(2,1)S(1)} %get-tuple-element.24.near_weight) | copy-start | bytes 12582916
  27.6 0.9 %copy-start.4 = (bf16[224,2048]{1,0:T(8,128)(2,1)}, bf16[224,2048]{1,0:T(8,128)(2,1)S(1)}, u32[]{:S(2)}) copy-start(bf16[224,2048]{1,0:T(8,128)(2,1)S(1)} %get-tuple-element.32) | copy-start | bytes 2752516
  28.5 15.5 %copy-start.3 = (bf16[2,512,2048]{2,1,0:T(8,128)(2,1)S(1)}, bf16[2,512,2048]{2,1,0:T(8,128)(2,1)}, u32[]{:S(2)}) copy-start(bf16[2,512,2048]{2,1,0:T(8,128)(2,1)} %copy-done.2) | copy-start | bytes 12582916
  31.7 1.9 %copy-start.5 = (bf16[224,2048]{1,0:T(8,128)(2,1)S(1)}, bf16[224,2048]{1,0:T(8,128)(2,1)}, u32[]{:S(2)}) copy-start(bf16[224,2048]{1,0:T(8,128)(2,1)} %copy-done.4) | copy-start | bytes 2752516
  31.7 12.4 %copy-start.1 = (bf16[512,4096]{1,0:T(8,128)(2,1)S(1)}, bf16[512,4096]{1,0:T(8,128)(2,1)}, u32[]{:S(2)}) copy-start(bf16[512,4096]{1,0:T(8,128)(2,1)} %copy-done) | copy-start | bytes 12582916
  32.9 13.4 %collective-permute-start.3 = (bf16[96,2048]{1,0:T(8,128)(2,1)S(1)}, bf16[96,2048]{1,0:T(8,128)(2,1)S(1)}, u32[]{:S(2)}, u32[]{:S(2)}) collective-permute-start(bf16[96,2048]{1,0:T(8,128)(2,1)S(1)} %add_convert_fusion.1), channel_id=1, source_target_pairs={{0,2},{1,3},{2,0},{3,1},{4,6},{5,7},{6,4},{7,5},{8,10},{9,11},{10,... | collective-permute-start | bytes 1179656 | tf_op jit(solution)/shard_map/ppermute | solution.py:411
  33.5 16.0 %collective-permute-start.6 = (bf16[224,2048]{1,0:T(8,128)(2,1)S(1)}, bf16[224,2048]{1,0:T(8,128)(2,1)S(1)}, u32[]{:S(2)}, u32[]{:S(2)}) collective-permute-start(bf16[224,2048]{1,0:T(8,128)(2,1)S(1)} %copy-done.5), channel_id=1, source_target_pairs={{0,1},{1,0},{2,3},{3,2},{4,5},{5,4},{6,7},{7,6},{8,9},{9,8},{10,11... | collective-permute-start | bytes 2752520 | tf_op jit(solution)/shard_map/ppermute | solution.py:503
  46.3 1.6 %collective-permute-start.4 = (bf16[64,2048]{1,0:T(8,128)(2,1)S(1)}, bf16[64,2048]{1,0:T(8,128)(2,1)S(1)}, u32[]{:S(2)}, u32[]{:S(2)}) collective-permute-start(bf16[64,2048]{1,0:T(8,128)(2,1)S(1)} %get-tuple-element.31), channel_id=1, source_target_pairs={{0,1},{1,0},{2,3},{3,2},{4,5},{5,4},{6,7},{7,6},{8,9},{9,8},{10,11... | collective-permute-start | bytes 786440 | tf_op jit(solution)/shard_map/ppermute | solution.py:522
  47.9 5.6 %collective-permute-start.5 = (bf16[32,2048]{1,0:T(8,128)(2,1)S(1)}, bf16[32,2048]{1,0:T(8,128)(2,1)S(1)}, u32[]{:S(2)}, u32[]{:S(2)}) collective-permute-start(bf16[32,2048]{1,0:T(8,128)(2,1)S(1)} %fusion), channel_id=1, source_target_pairs={{0,2},{1,3},{2,0},{3,1},{4,6},{5,7},{6,4},{7,5},{8,10},{9,11},{10,... | collective-permute-start | bytes 393224 | tf_op jit(solution)/shard_map/ppermute | solution.py:411
